TPU v7x, 32 devices: a whole 2x2x4 slice. The times are simulated.
32 devices in a mesh: wide: 8 (over z, y), narrow: 4 (over x, core).
Axes of the slice: x: 2, y: 2, z: 4, core: 2. Of those that a mesh axis runs over, the one named last changes fastest.
Arguments:
- inputs: bfloat16 [768, 12288], P('narrow', 'wide'), may hold values from -50 to 50
- clip_bounds: int32 [2, 12288], P(None, 'wide'), may hold values from 0 to 12288, as said below
- qkv_weight: bfloat16 [2, 3, 768, 768], P(None, None, 'wide', 'narrow'), may hold values from -0.21875 to 0.21875
- out_weight: bfloat16 [2, 768, 768], P(None, 'narrow', 'wide'), may hold values from -0.875 to 0.875
- fc1_weight: bfloat16 [2, 768, 3072], P(None, 'wide', 'narrow'), may hold values from -0.21875 to 0.21875
- fc2_weight: bfloat16 [2, 3072, 768], P(None, 'narrow', 'wide'), may hold values from -0.109375 to 0.109375
- gains: bfloat16 [2, 2, 768], P(None, None, ('narrow', 'wide')), may hold values from 0.25 to 1.75
- biases: bfloat16 [2, 6, 768], P(None, None, ('narrow', 'wide')), may hold values from -2 to 2
- fc1_bias: bfloat16 [2, 3072], P(None, ('narrow', 'wide')), may hold values from -2 to 2
- cotangent: bfloat16 [768, 12288], P('narrow', 'wide'), may hold values from -6 to 6
Outputs:
- activations: bfloat16 [768, 12288], P('narrow', 'wide')
- grad_input: float32 [768, 12288], P('narrow', 'wide')
- grad_qkv: float32 [2, 3, 768, 768], P(None, None, 'wide', 'narrow')
- grad_out: float32 [2, 768, 768], P(None, 'narrow', 'wide')
- grad_fc1: float32 [2, 768, 3072], P(None, 'wide', 'narrow')
- grad_fc2: float32 [2, 3072, 768], P(None, 'narrow', 'wide')
- grad_gains: float32 [2, 2, 768], P(None, None, ('narrow', 'wide'))
- grad_biases: float32 [2, 6, 768], P(None, None, ('narrow', 'wide'))
- grad_fc1_bias: float32 [2, 3072], P(None, ('narrow', 'wide'))
Inputs may be any that keep to these rules, and one draw needn't show every extreme that they name: `clip_bounds`: row 0 is each token's clip start and row 1 its clip end (exclusive). Clips are consecutive runs of tokens that cover all 12288 tokens, each of 1 to 1500 tokens; every clip but the first and the last has 750 tokens or more, and some clip has exactly 1500.
All inputs are finite; a program needn't handle non-finite values.
Results may differ from a plain program's by a relative error of at most 0.015.
Values may be sent and summed in bfloat16 or wider, within the bound.
No kernel may reach another device: no remote copies, remote signals or barrier semaphores. Data moves between devices by JAX's collectives and lax.ppermute only.
A program may use at most 256 MiB of HBM per device.

v0:
```python
import jax
import jax.numpy as jnp
from jax import lax
from jax.sharding import PartitionSpec as P

D = 768
HEAD_DIM = 64


EPSILON = 1e-05
MASKED = -1000000000.0
ROOT_HALF = 0.7071067811865476
INV_ROOT_TAU = 0.3989422804014327


def extended(cells, sides, width):
    for axis, dim in sides:
        count = lax.axis_size(axis)
        ends = count - 1
        head = lax.slice_in_dim(cells, 0, width, axis=dim)
        tail = lax.slice_in_dim(cells, cells.shape[dim] - width, cells.shape[dim], axis=dim)
        cells = jnp.concatenate(
            [
                lax.ppermute(tail, axis, [(i, (i + 1) % count) for i in range(ends)]),
                cells,
                lax.ppermute(head, axis, [((i + 1) % count, i) for i in range(ends)]),
            ],
            axis=dim,
        )
    return cells


def passed_along(value, axis, steps):
    count = lax.axis_size(axis)
    first, last = (max(0, -steps), min(count, count - steps))
    return lax.ppermute(value, axis, [(source, source + steps) for source in range(first, last)])


def gelu_slope(hidden):
    return (
        0.5 * (1.0 + lax.erf(hidden * ROOT_HALF))
        + hidden * jnp.exp(-0.5 * hidden * hidden) * INV_ROOT_TAU
    )


def norm_forward(values, gain_row, shift_row):
    center = lax.psum(jnp.sum(values, 1), "narrow") / D
    offset = values - center[:, None]
    spread = lax.psum(jnp.sum(offset * offset, 1), "narrow") / D
    inv_spread = lax.rsqrt(spread + EPSILON)
    normed = (values - center[:, None]) * inv_spread[:, None]
    rounded = (normed * gain_row + shift_row).astype(jnp.bfloat16)
    whole_rows = lax.all_gather(rounded, "narrow", axis=1, tiled=True)
    return (whole_rows, normed, inv_spread)


def norm_backward(upstream, normed, inv_spread, gain_row):
    scaled = upstream * gain_row
    first_sum, second_sum = lax.psum((jnp.sum(scaled, 1), jnp.sum(scaled * normed, 1)), "narrow")
    grad_values = inv_spread[:, None] * (
        scaled - first_sum[:, None] / D - normed * (second_sum[:, None] / D)
    )
    return (grad_values, jnp.sum(upstream * normed, 0), jnp.sum(upstream, 0))


def branch_total(partial_sum):
    return lax.psum_scatter(
        partial_sum.astype(jnp.bfloat16), "narrow", scatter_dimension=1, tiled=True
    ).astype(jnp.float32)


def input_total(partial_sum):
    return lax.psum_scatter(
        partial_sum.astype(jnp.bfloat16), "narrow", scatter_dimension=1, tiled=True
    ).astype(jnp.float32)


def branch_spread(gradient):
    return lax.all_gather(gradient.astype(jnp.bfloat16), "narrow", axis=1, tiled=True)


def masked_scores(query_block, key_rows, clip_start, clip_end, key_pos, score_scale):
    scores = (
        jnp.einsum("qhd,khd->hqk", query_block, key_rows, preferred_element_type=jnp.float32)
        * score_scale
    )
    inside = (key_pos[None, :] >= clip_start[:, None]) & (key_pos[None, :] < clip_end[:, None])
    return jnp.where(inside[None], scores, MASKED)


def attend_forward(queries, key_rows, value_rows, clip_starts, clip_ends, key_pos, score_scale):

    def attend_one(block_data):
        query_block, clip_start, clip_end = block_data
        scores = masked_scores(query_block, key_rows, clip_start, clip_end, key_pos, score_scale)
        row_peak = jnp.max(scores, -1, keepdims=True)
        weights_exp = jnp.exp(scores - row_peak)
        row_total = jnp.sum(weights_exp, -1, keepdims=True)
        probabilities = (weights_exp / row_total).astype(jnp.bfloat16)
        mixed_heads = jnp.einsum(
            "hqk,khd->qhd", probabilities, value_rows, preferred_element_type=jnp.float32
        )
        return (mixed_heads, (row_peak + jnp.log(row_total))[..., 0])

    return lax.map(attend_one, (queries, clip_starts, clip_ends))


def attend_backward(
    queries, grad_heads, logsums, clip_starts, clip_ends, key_rows, value_rows, key_pos, score_scale
):

    def back_step(carried, block_data):
        key_grad, value_grad = carried
        query_block, grad_block, logsum_block, clip_start, clip_end = block_data
        scores = masked_scores(query_block, key_rows, clip_start, clip_end, key_pos, score_scale)
        probabilities = jnp.exp(scores - logsum_block[..., None])
        prob_low = probabilities.astype(jnp.bfloat16)
        prob_grad = jnp.einsum(
            "qhd,khd->hqk", grad_block, value_rows, preferred_element_type=jnp.float32
        )
        inner_sum = jnp.sum(probabilities * prob_grad, -1, keepdims=True)
        score_grad = (probabilities * (prob_grad - inner_sum)).astype(jnp.bfloat16)
        query_grad = (
            jnp.einsum("hqk,khd->qhd", score_grad, key_rows, preferred_element_type=jnp.float32)
            * score_scale
        )
        key_grad = (
            key_grad
            + jnp.einsum(
                "hqk,qhd->khd", score_grad, query_block, preferred_element_type=jnp.float32
            )
            * score_scale
        )
        value_grad = value_grad + jnp.einsum(
            "hqk,qhd->khd", prob_low, grad_block, preferred_element_type=jnp.float32
        )
        return ((key_grad, value_grad), query_grad)

    zeros_kv = jnp.zeros(key_rows.shape, jnp.float32)
    return lax.scan(
        back_step, (zeros_kv, zeros_kv), (queries, grad_heads, logsums, clip_starts, clip_ends)
    )


def local(
    inputs,
    clip_bounds,
    qkv_weight,
    out_weight,
    fc1_weight,
    fc2_weight,
    gains,
    biases,
    fc1_bias,
    cotangent,
):
    tok_rows = inputs.shape[1]
    layers = qkv_weight.shape[0]
    heads_here = inputs.shape[0] // HEAD_DIM
    query_rows = min(512, tok_rows)
    block_count = tok_rows // query_rows
    score_scale = HEAD_DIM ** (-0.5)
    key_pos = (
        lax.axis_index("wide") * tok_rows - tok_rows + jnp.arange(3 * tok_rows, dtype=jnp.int32)
    )
    clip_starts = clip_bounds[0].reshape(block_count, query_rows)
    clip_ends = clip_bounds[1].reshape(block_count, query_rows)
    residual = inputs.astype(jnp.float32).T
    saved_state = []
    for layer_idx in range(layers):
        fetched = (
            lax.all_gather(qkv_weight[layer_idx], "wide", axis=1, tiled=True),
            lax.all_gather(out_weight[layer_idx], "wide", axis=1, tiled=True),
            lax.all_gather(fc1_weight[layer_idx], "wide", axis=0, tiled=True),
            lax.all_gather(fc2_weight[layer_idx], "wide", axis=1, tiled=True),
            lax.all_gather(gains[layer_idx], "wide", axis=1, tiled=True),
            lax.all_gather(biases[layer_idx], "wide", axis=1, tiled=True),
            lax.all_gather(fc1_bias[layer_idx], "wide", axis=0, tiled=True),
        )
        w_qkv, w_out, w_up, w_down, gain_pair, bias_rows, up_bias = fetched
        gain_pair = gain_pair.astype(jnp.float32)
        bias_rows = bias_rows.astype(jnp.float32)
        up_bias = up_bias.astype(jnp.float32)
        whole_one, normed_one, spread_one = norm_forward(residual, gain_pair[0], bias_rows[0])
        projected = jnp.einsum("td,kdc->ktc", whole_one, w_qkv, preferred_element_type=jnp.float32)
        offsets = jnp.stack([bias_rows[1], jnp.zeros_like(bias_rows[1]), bias_rows[2]])
        qkv_low = (projected + offsets[:, None, :]).astype(jnp.bfloat16)
        neighbours = extended(qkv_low[1:], (("wide", 1),), tok_rows)
        key_rows = neighbours[0].reshape(3 * tok_rows, heads_here, HEAD_DIM)
        value_rows = neighbours[1].reshape(3 * tok_rows, heads_here, HEAD_DIM)
        queries = qkv_low[0].reshape(block_count, query_rows, heads_here, HEAD_DIM)
        mixed_heads, logsums = attend_forward(
            queries, key_rows, value_rows, clip_starts, clip_ends, key_pos, score_scale
        )
        heads_low = mixed_heads.reshape(tok_rows, -1).astype(jnp.bfloat16)
        attention = (
            branch_total(jnp.dot(heads_low, w_out, preferred_element_type=jnp.float32))
            + bias_rows[3]
        )
        middle = residual + attention
        whole_two, normed_two, spread_two = norm_forward(middle, gain_pair[1], bias_rows[4])
        hidden = jnp.dot(whole_two, w_up, preferred_element_type=jnp.float32) + up_bias
        active = jax.nn.gelu(hidden, approximate=False).astype(jnp.bfloat16)
        residual = (
            middle
            + branch_total(jnp.dot(active, w_down, preferred_element_type=jnp.float32))
            + bias_rows[5]
        )
        saved_state.append(
            (
                fetched,
                whole_one,
                normed_one,
                spread_one,
                key_rows,
                value_rows,
                queries,
                logsums,
                heads_low,
                whole_two,
                normed_two,
                spread_two,
                hidden,
                active,
            )
        )
    gradient = cotangent.astype(jnp.float32).T
    results = []
    for layer_idx in reversed(range(layers)):
        (
            fetched,
            whole_one,
            normed_one,
            spread_one,
            key_rows,
            value_rows,
            queries,
            logsums,
            heads_low,
            whole_two,
            normed_two,
            spread_two,
            hidden,
            active,
        ) = saved_state[layer_idx]
        fetched = (
            lax.all_gather(qkv_weight[layer_idx], "wide", axis=1, tiled=True),
            lax.all_gather(out_weight[layer_idx], "wide", axis=1, tiled=True),
            lax.all_gather(fc1_weight[layer_idx], "wide", axis=0, tiled=True),
            lax.all_gather(fc2_weight[layer_idx], "wide", axis=1, tiled=True),
            lax.all_gather(gains[layer_idx], "wide", axis=1, tiled=True),
            lax.all_gather(biases[layer_idx], "wide", axis=1, tiled=True),
            lax.all_gather(fc1_bias[layer_idx], "wide", axis=0, tiled=True),
        )
        w_qkv, w_out, w_up, w_down, gain_pair, bias_rows, up_bias = fetched
        gain_pair = gain_pair.astype(jnp.float32)
        spread_mlp = branch_spread(gradient)
        grad_down_bias = jnp.sum(gradient, 0)
        grad_active = jnp.einsum(
            "td,fd->tf", spread_mlp, w_down, preferred_element_type=jnp.float32
        )
        grad_hidden = (grad_active * gelu_slope(hidden)).astype(jnp.bfloat16)
        grad_down = jnp.einsum("tf,td->fd", active, spread_mlp, preferred_element_type=jnp.float32)
        grad_up = jnp.einsum(
            "td,tf->df", whole_two, grad_hidden, preferred_element_type=jnp.float32
        )
        grad_up_bias = jnp.sum(grad_hidden.astype(jnp.float32), 0)
        normed_grad_two = input_total(
            jnp.einsum("tf,df->td", grad_hidden, w_up, preferred_element_type=jnp.float32)
        )
        back_two, gain_two, shift_two = norm_backward(
            normed_grad_two, normed_two, spread_two, gain_pair[1]
        )
        gradient = gradient + back_two
        spread_attn = branch_spread(gradient)
        grad_out_bias = jnp.sum(gradient, 0)
        grad_heads = jnp.einsum(
            "td,cd->tc", spread_attn, w_out, preferred_element_type=jnp.float32
        ).astype(jnp.bfloat16)
        grad_outw = jnp.einsum(
            "tc,td->cd", heads_low, spread_attn, preferred_element_type=jnp.float32
        )
        grad_blocks = grad_heads.reshape(block_count, query_rows, heads_here, HEAD_DIM)
        (key_grad, value_grad), query_grad = attend_backward(
            queries,
            grad_blocks,
            logsums,
            clip_starts,
            clip_ends,
            key_rows,
            value_rows,
            key_pos,
            score_scale,
        )
        halo_grads = jnp.stack(
            [key_grad.reshape(3 * tok_rows, -1), value_grad.reshape(3 * tok_rows, -1)]
        )
        from_upper = passed_along(halo_grads[:, :tok_rows].astype(jnp.bfloat16), "wide", -1).astype(
            jnp.float32
        )
        from_lower = passed_along(
            halo_grads[:, 2 * tok_rows :].astype(jnp.bfloat16), "wide", 1
        ).astype(jnp.float32)
        own_grads = halo_grads[:, tok_rows : 2 * tok_rows] + from_upper + from_lower
        grad_qkv_low = jnp.concatenate([query_grad.reshape(1, tok_rows, -1), own_grads]).astype(
            jnp.bfloat16
        )
        grad_qkvw = jnp.einsum(
            "td,ktc->kdc", whole_one, grad_qkv_low, preferred_element_type=jnp.float32
        )
        summed_qkv = jnp.sum(grad_qkv_low.astype(jnp.float32), 1)
        normed_grad_one = input_total(
            jnp.einsum("ktc,kdc->td", grad_qkv_low, w_qkv, preferred_element_type=jnp.float32)
        )
        back_one, gain_one, shift_one = norm_backward(
            normed_grad_one, normed_one, spread_one, gain_pair[0]
        )
        gradient = gradient + back_one
        gain_grads = jnp.stack([gain_one, gain_two])
        bias_grads = jnp.stack(
            [shift_one, summed_qkv[0], summed_qkv[2], grad_out_bias, shift_two, grad_down_bias]
        )
        shares = (
            lax.psum_scatter(grad_qkvw, "wide", scatter_dimension=1, tiled=True),
            lax.psum_scatter(grad_outw, "wide", scatter_dimension=1, tiled=True),
            lax.psum_scatter(grad_up, "wide", scatter_dimension=0, tiled=True),
            lax.psum_scatter(grad_down, "wide", scatter_dimension=1, tiled=True),
            lax.psum_scatter(gain_grads, "wide", scatter_dimension=1, tiled=True),
            lax.psum_scatter(bias_grads, "wide", scatter_dimension=1, tiled=True),
            lax.psum_scatter(grad_up_bias, "wide", scatter_dimension=0, tiled=True),
        )
        results.append(shares)
    results = results[::-1]
    stacked = [jnp.stack([entry[member] for entry in results]) for member in range(7)]
    return (
        residual.T.astype(jnp.bfloat16),
        gradient.T,
        stacked[0],
        stacked[1],
        stacked[2],
        stacked[3],
        stacked[4],
        stacked[5],
        stacked[6],
    )


def solution(mesh):
    in_specs = (
        P("narrow", "wide"),
        P(None, "wide"),
        P(None, None, "wide", "narrow"),
        P(None, "narrow", "wide"),
        P(None, "wide", "narrow"),
        P(None, "narrow", "wide"),
        P(None, None, ("narrow", "wide")),
        P(None, None, ("narrow", "wide")),
        P(None, ("narrow", "wide")),
        P("narrow", "wide"),
    )
    out_specs = (
        P("narrow", "wide"),
        P("narrow", "wide"),
        P(None, None, "wide", "narrow"),
        P(None, "narrow", "wide"),
        P(None, "wide", "narrow"),
        P(None, "narrow", "wide"),
        P(None, None, ("narrow", "wide")),
        P(None, None, ("narrow", "wide")),
        P(None, ("narrow", "wide")),
    )
    return jax.shard_map(local, mesh=mesh, in_specs=in_specs, out_specs=out_specs, check_vma=False)
```

profile of v0, /device:TPU:0, one launch (start us, length us, event | category | flops | bytes accessed | tf_op | source)
XLA Modules:
  0.0 2284.0 jit_solution(18342917775542414378)
XLA Ops:
  27.2 31.0 %all-gather = bf16[1,2,192]{1,0,2:T(2,128)(2,1)S(1)} all-gather(bf16[1,2,24]{1,0,2:T(2,128)(2,1)S(1)} %copy.107), channel_id=2, replica_groups=mesh['wide'=8,'narrow'=4] {'wide'}, dimensions={2}, use_global_device_ids=true | all-gather | bytes 864 | tf_op jit(solution)/shard_map/all_gather | solution.py:176
  61.8 30.5 %all-gather.1 = bf16[1,6,192]{1,0,2:T(2,128)(2,1)S(1)} all-gather(bf16[1,6,24]{1,0,2:T(2,128)(2,1)S(1)} %copy.108), channel_id=3, replica_groups=mesh['wide'=8,'narrow'=4] {'wide'}, dimensions={2}, use_global_device_ids=true | all-gather | bytes 2592 | tf_op jit(solution)/shard_map/all_gather | solution.py:177
  98.1 30.8 %all-gather.8 = bf16[1,6,192]{1,0,2:T(2,128)(2,1)S(1)} all-gather(bf16[1,6,24]{1,0,2:T(2,128)(2,1)S(1)} %copy.112), channel_id=10, replica_groups=mesh['wide'=8,'narrow'=4] {'wide'}, dimensions={2}, use_global_device_ids=true | all-gather | bytes 2592 | tf_op jit(solution)/shard_map/all_gather | solution.py:177
  129.8 45.8 %all-gather.2 = bf16[1,3,768,192]{3,1,0,2:T(4,128)(2,1)S(1)} all-gather(bf16[1,3,96,192]{3,1,0,2:T(4,128)(2,1)S(1)} %copy.106), channel_id=4, replica_groups=mesh['wide'=8,'narrow'=4] {'wide'}, dimensions={2}, use_global_device_ids=true | all-gather | bytes 995328 | tf_op jit(solution)/shard_map/all_gather | solution.py:172
  192.9 54.3 %all-gather.3 = bf16[1,192,768]{1,0,2:T(2,128)(2,1)} all-gather(bf16[1,192,96]{1,0,2:T(2,128)(2,1)S(1)} %copy.109), channel_id=5, replica_groups=mesh['wide'=8,'narrow'=4] {'wide'}, dimensions={2}, use_global_device_ids=true | all-gather | bytes 331776 | tf_op jit(solution)/shard_map/all_gather | solution.py:173
  255.9 131.3 %while.56 = (s32[]{:T(128)}, bf16[3,512,3,64]{1,3,2,0:T(8,128)(2,1)S(1)}, f32[3,3,512]{2,1,0:T(4,128)}, s32[3,512]{1,0:T(4,128)S(1)}, s32[3,512]{1,0:T(4,128)S(1...) while((s32[]{:T(128)}, ...), condition=%wide.region_7.8_spmd.clone, body=%wide.region_4.7_spmd.clone.sunk | while | flops 1903954944 | bytes 98605176 | solution.py:105
  479.1 29.6 %all-gather.45.cloned.1.call-done = bf16[1,768,768]{1,2,0:T(8,128)(2,1)} async-done(((bf16[1,768,96]{1,2,0:T(8,128)(2,1)}), bf16[1,768,768]{1,2,0:T(8,128)(2,1)}) %all-gather.45.cloned.1.call-update) | async-done | bytes 1179664 | tf_op jit(solution)/shard_map/all_gather | solution.py:175
  514.9 30.5 %all-gather.7 = bf16[1,2,192]{1,0,2:T(2,128)(2,1)S(1)} all-gather(bf16[1,2,24]{1,0,2:T(2,128)(2,1)S(1)} %copy.111), channel_id=9, replica_groups=mesh['wide'=8,'narrow'=4] {'wide'}, dimensions={2}, use_global_device_ids=true | all-gather | bytes 864 | tf_op jit(solution)/shard_map/all_gather | solution.py:176
  564.7 35.6 %all-gather.9 = bf16[1,3,768,192]{3,1,0,2:T(4,128)(2,1)S(1)} all-gather(bf16[1,3,96,192]{3,1,0,2:T(4,128)(2,1)S(1)} %copy.110), channel_id=11, replica_groups=mesh['wide'=8,'narrow'=4] {'wide'}, dimensions={2}, use_global_device_ids=true | all-gather | bytes 995328 | tf_op jit(solution)/shard_map/all_gather | solution.py:172
  613.3 71.3 %all-gather.10 = bf16[1,192,768]{1,0,2:T(2,128)(2,1)} all-gather(bf16[1,192,96]{1,0,2:T(2,128)(2,1)S(1)} %copy.113), channel_id=12, replica_groups=mesh['wide'=8,'narrow'=4] {'wide'}, dimensions={2}, use_global_device_ids=true | all-gather | bytes 331776 | tf_op jit(solution)/shard_map/all_gather | solution.py:173
  693.4 131.7 %while.57 = (s32[]{:T(128)}, bf16[3,512,3,64]{1,3,2,0:T(8,128)(2,1)S(1)}, f32[3,3,512]{2,1,0:T(4,128)}, s32[3,512]{1,0:T(4,128)S(1)}, s32[3,512]{1,0:T(4,128)S(1...) while((s32[]{:T(128)}, ...), condition=%wide.region_21.22_spmd.clone, body=%wide.region_18.21_spmd.clone.sunk | while | flops 1903954944 | bytes 98605176 | solution.py:105
  829.3 30.4 %reduce-scatter.33.cloned.1.call-done = bf16[1536,192]{0,1:T(8,128)(2,1)} async-done(((bf16[1536,768]{0,1:T(8,128)(2,1)}), bf16[1536,192]{0,1:T(8,128)(2,1)}) %reduce-scatter.33.cloned.1.call-update) | async-done | bytes 589840 | tf_op jit(solution)/shard_map/reduce_scatter | solution.py:67
  914.4 29.0 %all-gather.49.cloned.1.call-done = bf16[1,768,768]{1,2,0:T(8,128)(2,1)} async-done(((bf16[1,768,96]{1,2,0:T(8,128)(2,1)}), bf16[1,768,768]{1,2,0:T(8,128)(2,1)}) %all-gather.49.cloned.1.call-update) | async-done | bytes 1179664 | tf_op jit(solution)/shard_map/all_gather | solution.py:175
  985.1 27.6 %reduce-scatter.37.cloned.1.call-done = bf16[1536,192]{0,1:T(8,128)(2,1)} async-done(((bf16[1536,768]{0,1:T(8,128)(2,1)}), bf16[1536,192]{0,1:T(8,128)(2,1)}) %reduce-scatter.37.cloned.1.call-update) | async-done | bytes 589840 | tf_op jit(solution)/shard_map/reduce_scatter | solution.py:73
  1082.0 305.1 %while.58 = (s32[]{:T(128)}, f32[4608,3,64]{0,2,1:T(8,128)}, f32[4608,3,64]{0,2,1:T(8,128)}, bf16[3,512,3,64]{1,3,2,0:T(8,128)(2,1)}, bf16[3,512,3,64]{1,3,2,0:T...) while((s32[]{:T(128)}, f32[4608,3,64]{0,2,1:T(8,128)}, ...), condition=%wide.region_35.36_spmd.clone, body=%wide.region_33.35_spmd.clone.sunk | while | flops 4647619584 | bytes 270821568 | solution.py:140
  1423.0 25.2 %collective-permute-done.5 = bf16[2,1536,192]{1,2,0:T(8,128)(2,1)} collective-permute-done((bf16[2,1536,192]{1,2,0:T(8,128)(2,1)}, bf16[2,1536,192]{1,2,0:T(8,128)(2,1)}, u32[]{:S(2)}, u32[]{:S(2)}) %collective-permute-start.5) | collective-permute-done | bytes 1179680 | tf_op jit(solution)/shard_map/ppermute | solution.py:36
  1455.2 33.2 %reduce-scatter.39.cloned.1.call-done = bf16[1536,192]{0,1:T(8,128)(2,1)} async-done(((bf16[1536,768]{0,1:T(8,128)(2,1)}), bf16[1536,192]{0,1:T(8,128)(2,1)}) %reduce-scatter.39.cloned.1.call-update) | async-done | bytes 589840 | tf_op jit(solution)/shard_map/reduce_scatter | solution.py:73
  1540.7 33.2 %reduce-scatter.41.cloned.1.call-done = bf16[1536,192]{0,1:T(8,128)(2,1)} async-done(((bf16[1536,768]{0,1:T(8,128)(2,1)}), bf16[1536,192]{0,1:T(8,128)(2,1)}) %reduce-scatter.41.cloned.1.call-update) | async-done | bytes 589840 | tf_op jit(solution)/shard_map/reduce_scatter | solution.py:73
  1636.6 307.9 %while.59 = (s32[]{:T(128)}, f32[4608,3,64]{0,2,1:T(8,128)}, f32[4608,3,64]{0,2,1:T(8,128)}, bf16[3,512,3,64]{1,3,2,0:T(8,128)(2,1)}, bf16[3,512,3,64]{1,3,2,0:T...) while((s32[]{:T(128)}, f32[4608,3,64]{0,2,1:T(8,128)}, ...), condition=%wide.region_48.49_spmd.clone, body=%wide.region_46.48_spmd.clone.sunk | while | flops 4647619584 | bytes 270821568 | solution.py:140
  1982.6 29.6 %collective-permute-done.7 = bf16[2,1536,192]{1,2,0:T(8,128)(2,1)} collective-permute-done((bf16[2,1536,192]{1,2,0:T(8,128)(2,1)}, bf16[2,1536,192]{1,2,0:T(8,128)(2,1)}, u32[]{:S(2)}, u32[]{:S(2)}) %collective-permute-start.7) | collective-permute-done | bytes 1179680 | tf_op jit(solution)/shard_map/ppermute | solution.py:36
  2054.8 63.4 %reduce-scatter.57.cloned.1.call-done = f32[96,192]{1,0:T(8,128)} async-done(((f32[768,192]{1,0:T(8,128)}), f32[96,192]{1,0:T(8,128)}) %reduce-scatter.57.cloned.1.call-update) | async-done | bytes 73744
  2120.3 67.5 %reduce-scatter.53.cloned.1.call-done = f32[96,576]{1,0:T(8,128)} async-done(((f32[768,576]{1,0:T(8,128)}), f32[96,576]{1,0:T(8,128)}) %reduce-scatter.53.cloned.1.call-update) | async-done | bytes 221200
  2190.3 32.1 %reduce-scatter.43.cloned.1.call-done = bf16[1536,192]{0,1:T(8,128)(2,1)} async-done(((bf16[1536,768]{0,1:T(8,128)(2,1)}), bf16[1536,192]{0,1:T(8,128)(2,1)}) %reduce-scatter.43.cloned.1.call-update) | async-done | bytes 589840 | tf_op jit(solution)/shard_map/reduce_scatter | solution.py:73
  2224.2 37.1 %all-reduce.8 = (f32[2,192]{1,0:T(2,128)S(1)}, f32[2,192]{1,0:T(2,128)S(1)}, f32[6,192]{1,0:T(8,128)S(1)}, f32[6,192]{1,0:T(8,128)S(1)}, f32[768]{0:T(1024)S(1)}, /*index=5*/f32[768]{0:T(1024)S(1)}) all-reduce(f32[2,192]{1,0:T(2,128)S(1)} %pad_maximum_fusion.18, ...), channel_id=33, replica_groups=mesh['wide'=8,'narrow'=4] {'wide'}, use_global_device_ids=true, to_apply=%region_67.68.clone | all-reduce | flops 4608 | bytes 36864
  (600 shorter events, 1495.1 us)
Async XLA Ops:
  8.0 173.6 %all-gather.27.cloned.1.call-start = ((), (), s32[]{:S(2)}) async-start(), calls=%async_computation.16 | async-start | bytes 2949120 | tf_op jit(solution)/shard_map/all_gather | solution.py:53
  97.9 325.0 %reduce-scatter.29.cloned.1.call-start = ((), (), s32[]{:S(2)}) async-start(), calls=%async_computation.17 | async-start | bytes 2949120 | tf_op jit(solution)/shard_map/reduce_scatter | solution.py:67
  391.0 72.7 %all-gather.43.cloned.1.call-start = ((), (), s32[]{:S(2)}) async-start(), calls=%async_computation.36 | async-start | bytes 1327104 | tf_op jit(solution)/shard_map/all_gather | solution.py:174
  391.8 72.5 %all-gather.29.cloned.1.call-start = ((), (), s32[]{:S(2)}) async-start(), calls=%async_computation.18 | async-start | bytes 2949120 | tf_op jit(solution)/shard_map/all_gather | solution.py:53
  439.7 109.5 %reduce-scatter.31.cloned.1.call-start = ((), (), s32[]{:S(2)}) async-start(), calls=%async_computation.19 | async-start | bytes 2949120 | tf_op jit(solution)/shard_map/reduce_scatter | solution.py:67
  514.2 88.2 %all-gather.31.cloned.1.call-start = ((), (), s32[]{:S(2)}) async-start(), calls=%async_computation.20 | async-start | bytes 2949120 | tf_op jit(solution)/shard_map/all_gather | solution.py:53
  564.5 295.2 %reduce-scatter.33.cloned.1.call-start = ((), (), s32[]{:S(2)}) async-start(), calls=%async_computation.21 | async-start | bytes 2949120 | tf_op jit(solution)/shard_map/reduce_scatter | solution.py:67
  606.3 82.6 %collective-permute-start.3 = (bf16[2,1536,192]{1,2,0:T(8,128)(2,1)S(1)}, bf16[2,1536,192]{1,2,0:T(8,128)(2,1)}, u32[]{:S(2)}, u32[]{:S(2)}) collective-permute-start(bf16[2,1536,192]{1,2,0:T(8,128)(2,1)S(1)} %slice.251), channel_id=1, source_target_pairs={{4,0},{8,4},{12,8},{16,12},{20,16},{24,20},{28,24},{5,1},{9,5},{13... | collective-permute-start | bytes 3538952 | tf_op jit(solution)/shard_map/ppermute | solution.py:26
  607.6 81.3 %collective-permute-start.2 = (bf16[2,1536,192]{1,2,0:T(8,128)(2,1)S(1)}, bf16[2,1536,192]{1,2,0:T(8,128)(2,1)}, u32[]{:S(2)}, u32[]{:S(2)}) collective-permute-start(bf16[2,1536,192]{1,2,0:T(8,128)(2,1)S(1)} %slice.251), channel_id=1, source_target_pairs={{0,4},{4,8},{8,12},{12,16},{16,20},{20,24},{24,28},{1,5},{5,9},{9,... | collective-permute-start | bytes 3538952 | tf_op jit(solution)/shard_map/ppermute | solution.py:24
  875.3 92.6 %all-gather.35.cloned.1.call-start = ((), (), s32[]{:S(2)}) async-start(), calls=%async_computation.24 | async-start | bytes 2949120 | tf_op jit(solution)/shard_map/all_gather | solution.py:79
  876.3 136.5 %reduce-scatter.37.cloned.1.call-start = ((), (), s32[]{:S(2)}) async-start(), calls=%async_computation.25 | async-start | bytes 2949120 | tf_op jit(solution)/shard_map/reduce_scatter | solution.py:73
  985.1 92.4 %all-gather.37.cloned.1.call-start = ((), (), s32[]{:S(2)}) async-start(), calls=%async_computation.26 | async-start | bytes 2949120 | tf_op jit(solution)/shard_map/all_gather | solution.py:79
  1053.4 435.0 %reduce-scatter.39.cloned.1.call-start = ((), (), s32[]{:S(2)}) async-start(), calls=%async_computation.27 | async-start | bytes 2949120 | tf_op jit(solution)/shard_map/reduce_scatter | solution.py:73
  1455.1 73.8 %all-gather.39.cloned.1.call-start = ((), (), s32[]{:S(2)}) async-start(), calls=%async_computation.28 | async-start | bytes 2949120 | tf_op jit(solution)/shard_map/all_gather | solution.py:79
  1540.6 90.5 %all-gather.41.cloned.1.call-start = ((), (), s32[]{:S(2)}) async-start(), calls=%async_computation.30 | async-start | bytes 2949120 | tf_op jit(solution)/shard_map/all_gather | solution.py:79
  1590.6 440.7 %reduce-scatter.59.cloned.1.call-start = ((), (), s32[]{:S(2)}) async-start(), calls=%async_computation.43 | async-start | bytes 884736
  1593.8 439.0 %reduce-scatter.55.cloned.1.call-start = ((), (), s32[]{:S(2)}) async-start(), calls=%async_computation.41 | async-start | bytes 2211840
  1604.8 429.5 %reduce-scatter.47.cloned.1.call-start = ((), (), s32[]{:S(2)}) async-start(), calls=%async_computation.33 | async-start | bytes 2654208 | tf_op jit(solution)/shard_map/reduce_scatter | solution.py:326
  1610.7 423.6 %reduce-scatter.45.cloned.1.call-start = ((), (), s32[]{:S(2)}) async-start(), calls=%async_computation.32 | async-start | bytes 2654208 | tf_op jit(solution)/shard_map/reduce_scatter | solution.py:326
  1617.5 418.8 %reduce-scatter.51.cloned.1.call-start = ((), (), s32[]{:S(2)}) async-start(), calls=%async_computation.35 | async-start | bytes 2654208 | tf_op jit(solution)/shard_map/reduce_scatter | solution.py:327
  1624.3 428.7 %reduce-scatter.49.cloned.1.call-start = ((), (), s32[]{:S(2)}) async-start(), calls=%async_computation.34 | async-start | bytes 2654208 | tf_op jit(solution)/shard_map/reduce_scatter | solution.py:327
  1631.1 487.2 %reduce-scatter.57.cloned.1.call-start = ((), (), s32[]{:S(2)}) async-start(), calls=%async_computation.42 | async-start | bytes 884736
  1958.6 229.3 %reduce-scatter.53.cloned.1.call-start = ((), (), s32[]{:S(2)}) async-start(), calls=%async_computation.40 | async-start | bytes 2211840
  2024.4 198.0 %reduce-scatter.43.cloned.1.call-start = ((), (), s32[]{:S(2)}) async-start(), calls=%async_computation.31 | async-start | bytes 2949120 | tf_op jit(solution)/shard_map/reduce_scatter | solution.py:73
  (121 other events, 4229.7 us)
Sparse Core Ops, SparseCore 0:
  98.0 24.0 all-gather.26
  391.1 31.7 reduce-scatter.28
  564.6 22.0 all-gather.30
  828.4 31.2 reduce-scatter.32
  979.7 33.0 reduce-scatter.36
  1015.1 33.0 reduce-scatter.34
  1455.3 33.1 reduce-scatter.38
  1540.8 33.0 reduce-scatter.40
Sparse Core Ops, SparseCore 1:
  394.4 40.2 all-gather.42
  438.9 25.3 all-gather.28
  467.2 41.5 all-gather.44
  514.3 31.4 reduce-scatter.30
  831.5 39.7 all-gather.46
  874.8 24.7 all-gather.32
  901.9 41.5 all-gather.48
  945.5 22.4 all-gather.34
  1053.5 23.9 all-gather.36
  1504.0 24.9 all-gather.38
  1590.7 24.9 all-gather.40
  1619.4 62.5 reduce-scatter.58
  1685.3 65.8 reduce-scatter.54
  1755.0 68.1 reduce-scatter.46
  1827.1 68.0 reduce-scatter.44
  1899.1 73.5 reduce-scatter.50
  1976.5 76.3 reduce-scatter.48
  2056.6 61.6 reduce-scatter.56
  2121.6 66.2 reduce-scatter.52
  2190.6 31.8 reduce-scatter.42
where the time goes:
time: 2300 us; the launch traced here: 2280 us
  matrix products  721 us (31%)
  waiting for transfers between devices  600 us (26%)
  blocking collectives  481 us (21%)
  other arithmetic  316 us (14%)
  local copies, waits for them, and re-layouts  106 us (5%)
  starting transfers between devices  38.9 us (2%)
    dot_general x12, matrix products, masked_scores(): jnp.einsum('qhd,khd->hqk', query_block, key_rows, preferred_element_type=...  171 us
    convert_element_type x6, other arithmetic, back_step(): score_grad = (probabilities * (prob_grad - inner_sum)).astype(jnp.bfloat16)  146 us
    dot_general x6, matrix products, back_step(): jnp.einsum('qhd,khd->hqk', grad_block, value_rows, preferred_element_type...  146 us
    unnamed x32, waiting for transfers between devices  133 us
    reduce_scatter x4, waiting for transfers between devices, input_total(): lax.psum_scatter(partial_sum.astype(jnp.bfloat16), 'narrow', scatter_dime...  126 us
    all_gather x2, blocking collectives, local(): lax.all_gather(out_weight[layer_idx], 'wide', axis=1, tiled=True)  126 us
    ppermute x4, waiting for transfers between devices, passed_along(): lax.ppermute(value, axis, [(source, source + steps) for source in range(f...  93.1 us
    dot_general x6, matrix products, back_step(): jnp.einsum('hqk,qhd->khd', prob_low, grad_block, preferred_element_type=j...  91.2 us
  transfers between devices with their start and end apart: 36, of which 21 were waited for; matrix products, arithmetic and copies ran while one was open for 20% of the time, Pallas kernels for 0%

commit v1 on v0

v1 whole, which is shorter than its diff:
```python
import functools

import jax
import jax.numpy as jnp
from jax import lax
from jax.sharding import PartitionSpec as P

EPSILON = 1e-05
ROOT_HALF = 0.7071067811865476
INV_ROOT_TAU = 0.3989422804014327
HEAD_DIM = 64
MASKED = -1e9


def contract(left, right, left_dim, right_dim):
    return lax.dot_general(
        left, right, (((left_dim,), (right_dim,)), ((), ())), preferred_element_type=jnp.float32
    )


def window_sizes(rows):
    return [size for size in (1152, 1664, 2176, 2688, 3200) if size < rows] + [rows]


def by_window(spans, rows, branch, operands):
    sizes = window_sizes(rows)
    first = spans[0] // 128 * 128
    needed = spans[1] - first
    choice = sum((needed > size).astype(jnp.int32) for size in sizes[:-1])
    return lax.switch(
        choice,
        [
            functools.partial(
                lambda size, *given: branch(size, jnp.clip(first, 0, rows - size), *given), size
            )
            for size in sizes
        ],
        *operands,
    )


def masked_scores(query_block, key_rows, starts, ends, first):
    scores = HEAD_DIM**-0.5 * jnp.einsum(
        "qhd,khd->hqk", query_block, key_rows, preferred_element_type=jnp.float32
    )
    positions = first + jnp.arange(key_rows.shape[0], dtype=jnp.int32)
    inside = (positions[None, :] >= starts[:, None]) & (positions[None, :] < ends[:, None])
    return jnp.where(inside[None], scores, MASKED)


def attend_forward(queries, key_rows, value_rows, bounds, spans):
    def one_block(data):
        query_block, starts, ends, span = data

        def branch(size, first, query_block, starts, ends):
            keys = lax.dynamic_slice_in_dim(key_rows, first, size, 0)
            values = lax.dynamic_slice_in_dim(value_rows, first, size, 0)
            scores = masked_scores(query_block, keys, starts, ends, first)
            peak = jnp.max(scores, -1, keepdims=True)
            weights = jnp.exp(scores - peak)
            total = jnp.sum(weights, -1, keepdims=True)
            probabilities = (weights / total).astype(jnp.bfloat16)
            mixed = jnp.einsum(
                "hqk,khd->qhd", probabilities, values, preferred_element_type=jnp.float32
            )
            return mixed, (peak + jnp.log(total))[..., 0]

        return by_window(span, key_rows.shape[0], branch, (query_block, starts, ends))

    return lax.map(one_block, (queries, bounds[0], bounds[1], spans))


def attend_backward(queries, grads, inner_sums, logsums, key_rows, value_rows, bounds, spans):
    def one_block(carried, data):
        query_block, grad_block, inner, logsum, starts, ends, span = data

        def branch(size, first, key_grad, value_grad, query_block, grad_block, inner, logsum, starts, ends):
            keys = lax.dynamic_slice_in_dim(key_rows, first, size, 0)
            values = lax.dynamic_slice_in_dim(value_rows, first, size, 0)
            scores = masked_scores(query_block, keys, starts, ends, first)
            weights = jnp.exp(scores - logsum[..., None])
            weight_grad = jnp.einsum(
                "qhd,khd->hqk", grad_block, values, preferred_element_type=jnp.float32
            )
            score_grad = (weights * (weight_grad - inner[..., None])).astype(jnp.bfloat16)
            query_grad = jnp.einsum(
                "hqk,khd->qhd", score_grad, keys, preferred_element_type=jnp.float32
            )
            key_part = jnp.einsum(
                "hqk,qhd->khd", score_grad, query_block, preferred_element_type=jnp.float32
            )
            value_part = jnp.einsum(
                "hqk,qhd->khd",
                weights.astype(jnp.bfloat16),
                grad_block,
                preferred_element_type=jnp.float32,
            )
            key_part = key_part + lax.dynamic_slice_in_dim(key_grad, first, size, 0)
            value_part = value_part + lax.dynamic_slice_in_dim(value_grad, first, size, 0)
            return (
                lax.dynamic_update_slice_in_dim(key_grad, key_part, first, 0),
                lax.dynamic_update_slice_in_dim(value_grad, value_part, first, 0),
                query_grad,
            )

        key_grad, value_grad, query_grad = by_window(
            span,
            key_rows.shape[0],
            branch,
            (*carried, query_block, grad_block, inner, logsum, starts, ends),
        )
        return (key_grad, value_grad), query_grad

    zeros = jnp.zeros(key_rows.shape, jnp.float32)
    return lax.scan(
        one_block,
        (zeros, zeros),
        (queries, grads, inner_sums, logsums, bounds[0], bounds[1], spans),
    )


def walk(place):
    pair, side = divmod(place, 2)
    return 2 * pair + (side + pair) % 2


def along_path(value, step):
    count = lax.axis_size("wide")
    first, last = max(0, -step), min(count, count - step)
    return lax.ppermute(
        value, "wide", [(walk(place), walk(place + step)) for place in range(first, last)]
    )


def swap_places(value):
    count = lax.axis_size("wide")
    return lax.ppermute(value, "wide", [(walk(place), place) for place in range(count)])


def partner(value, mask):
    return lax.ppermute(value, "narrow", [(i, i ^ mask) for i in range(4)])


def gather_tokens(part):
    narrow = lax.axis_index("narrow")
    core, column = narrow % 2, narrow // 2
    across = partner(part, 2)
    both = jnp.stack([part, across])
    beside = partner(both, 1)
    mine = jnp.where(column == 0, both, both[::-1])
    other = jnp.where(column == 0, beside, beside[::-1])
    low = jnp.where(core == 0, mine, other)
    high = jnp.where(core == 0, other, mine)
    return jnp.concatenate([low[0], high[0], low[1], high[1]], axis=1)


def scatter_tokens(partial):
    narrow = lax.axis_index("narrow")
    core, column = narrow % 2, narrow // 2
    rows = partial.shape[1] // 4
    blocks = [partial[:, i * rows : (i + 1) * rows] for i in range(4)]
    even = jnp.stack([blocks[0], blocks[2]])
    odd = jnp.stack([blocks[1], blocks[3]])
    keep = jnp.where(core == 0, even, odd)
    give = jnp.where(core == 0, odd, even)
    taken = partner(give.astype(jnp.bfloat16), 1)
    pair = keep.astype(jnp.float32) + taken.astype(jnp.float32)
    keep = jnp.where(column == 0, pair[0], pair[1])
    give = jnp.where(column == 0, pair[1], pair[0])
    return keep + partner(give.astype(jnp.bfloat16), 2).astype(jnp.float32)


def swapped(value, axis, mask):
    count = lax.axis_size(axis)
    return lax.ppermute(value, axis, [(i, i ^ mask) for i in range(count)])


def gather_blocks(value, axis):
    place = 0
    mask = lax.axis_size(axis) // 2
    while mask:
        other = swapped(value, axis, mask)
        upper = (lax.axis_index(axis) & mask) != 0
        value = jnp.stack(
            [jnp.where(upper, other, value), jnp.where(upper, value, other)], axis=place
        )
        place += 1
        mask //= 2
    return value.reshape((-1,) + value.shape[place:])


def scatter_blocks(value, axis, sent):
    count = lax.axis_size(axis)
    mask = 1
    while mask < count:
        value = value.reshape((-1, 2) + value.shape[1:])
        upper = (lax.axis_index(axis) & mask) != 0
        give = jnp.where(upper, value[:, 0], value[:, 1]).astype(sent)
        keep = jnp.where(upper, value[:, 1], value[:, 0])
        value = keep.astype(jnp.float32) + swapped(give, axis, mask).astype(jnp.float32)
        mask *= 2
    return value[0]


def ordered(blocks):
    narrow = lax.axis_index("narrow")
    core, column = narrow % 2 == 1, narrow // 2 == 1
    near = [jnp.where(core, blocks[i ^ 1], blocks[i]) for i in range(4)]
    return [jnp.where(column, near[i ^ 2], near[i]) for i in range(4)]


def exchange(blocks):
    count = lax.axis_size("wide")
    received = []
    for mask, block in enumerate(ordered(blocks)):
        pairs = [(4 * w + n, 4 * walk(w) + (n ^ mask)) for w in range(count) for n in range(4)]
        received.append(lax.ppermute(block, ("wide", "narrow"), pairs))
    return ordered(received)


def features_to_tokens(value):
    rows = value.shape[1] // 4
    return jnp.concatenate(
        exchange([value[:, i * rows : (i + 1) * rows] for i in range(4)]), axis=0
    )


def tokens_to_features(value):
    rows = value.shape[0] // 4
    return jnp.concatenate(exchange([value[i * rows : (i + 1) * rows] for i in range(4)]), axis=1)


def gelu_slope(hidden):
    return (
        0.5 * (1.0 + lax.erf(hidden * ROOT_HALF))
        + hidden * jnp.exp(-0.5 * hidden * hidden) * INV_ROOT_TAU
    )


def norm_forward(values, gain, shift):
    offset = values - jnp.mean(values, 0, keepdims=True)
    inverse = lax.rsqrt(jnp.mean(offset * offset, 0, keepdims=True) + EPSILON)
    normed = offset * inverse
    return (normed * gain[:, None] + shift[:, None]).astype(jnp.bfloat16), normed, inverse


def norm_backward(upstream, normed, inverse, gain):
    scaled = upstream * gain[:, None]
    grad = inverse * (
        scaled
        - jnp.mean(scaled, 0, keepdims=True)
        - normed * jnp.mean(scaled * normed, 0, keepdims=True)
    )
    return grad, jnp.sum(upstream * normed, 1), jnp.sum(upstream, 1)


def local(
    inputs,
    clip_bounds,
    qkv_weight,
    out_weight,
    fc1_weight,
    fc2_weight,
    gains,
    biases,
    fc1_bias,
    cotangent,
):
    layers = qkv_weight.shape[0]
    width_here, tokens = inputs.shape
    d_model = 4 * width_here
    wide_count = lax.axis_size("wide")
    narrow = lax.axis_index("narrow")
    wide = lax.axis_index("wide")
    place = 2 * (wide // 2) + (wide + wide // 2) % 2
    devices = 4 * wide_count

    qkv_weights, other_weights = [], []
    for layer in range(layers):
        shard = qkv_weight[layer].transpose(1, 0, 2).reshape(-1, 3 * width_here)
        qkv_weights.append(gather_blocks(shard, "wide").reshape(d_model, -1))
        shard = jnp.concatenate(
            [fc1_weight[layer], fc2_weight[layer].T, out_weight[layer].T], axis=1
        )
        other_weights.append(gather_blocks(shard, "wide").reshape(d_model, -1))
    hidden_here = fc1_weight.shape[2]

    vectors = jnp.concatenate([gains.reshape(-1), biases.reshape(-1), fc1_bias.reshape(-1)])
    vectors = vectors.astype(jnp.float32)
    vectors = gather_blocks(vectors, "wide")
    vectors = gather_blocks(vectors, "narrow").reshape(devices, -1)
    gain_size, bias_size = gains.size, biases.size

    def whole(columns, rows):
        return columns.reshape(devices, layers, rows, -1).transpose(1, 2, 0, 3).reshape(
            layers, rows, d_model
        )

    gain_all = whole(vectors[:, :gain_size], 2)
    bias_all = whole(vectors[:, gain_size : gain_size + bias_size], 6)
    up_bias = (
        vectors[:, gain_size + bias_size :]
        .reshape(4, wide_count, layers, -1)
        .transpose(2, 0, 1, 3)
        .reshape(layers, 4, hidden_here)
    )
    up_bias = lax.dynamic_index_in_dim(up_bias, narrow, 1, False)

    q_tile = 512 if tokens % 512 == 0 else tokens
    heads_here = width_here // HEAD_DIM
    bounds = swap_places(clip_bounds) - (place - 1) * tokens
    bounds = bounds.reshape(2, -1, q_tile)
    spans = jnp.stack([bounds[0, :, 0], bounds[1, :, -1]], axis=1)

    def head_blocks(value):
        return value.reshape(-1, q_tile, heads_here, HEAD_DIM)


    residual = features_to_tokens(inputs).astype(jnp.float32)
    saved = []
    for layer in range(layers):
        bias = bias_all[layer]
        w_qkv = qkv_weights[layer]
        own_bias = lax.dynamic_slice_in_dim(bias, narrow * width_here, width_here, 1)
        low_one, normed_one, inverse_one = norm_forward(residual, gain_all[layer, 0], bias[0])
        whole_one = gather_tokens(low_one)
        kv = contract(whole_one, w_qkv[:, width_here:], 0, 0)
        kv = kv + jnp.concatenate([jnp.zeros_like(own_bias[2]), own_bias[2]])
        kv = kv.astype(jnp.bfloat16)
        kv = jnp.concatenate([along_path(kv, 1), kv, along_path(kv, -1)])
        key_rows = kv[:, :width_here].reshape(-1, heads_here, HEAD_DIM)
        value_rows = kv[:, width_here:].reshape(-1, heads_here, HEAD_DIM)
        queries = contract(whole_one, w_qkv[:, :width_here], 0, 0) + own_bias[1]
        queries = head_blocks(queries.astype(jnp.bfloat16))
        heads, logsum = attend_forward(queries, key_rows, value_rows, bounds, spans)
        low_heads = heads.reshape(tokens, width_here).astype(jnp.bfloat16)
        w_other = other_weights[layer]
        w_up, w_down, w_out = (
            w_other[:, :hidden_here],
            w_other[:, hidden_here : 2 * hidden_here],
            w_other[:, 2 * hidden_here :],
        )
        attention = scatter_tokens(contract(w_out, low_heads, 1, 1))
        middle = residual + attention + bias[3][:, None]
        low_two, normed_two, inverse_two = norm_forward(middle, gain_all[layer, 1], bias[4])
        whole_two = gather_tokens(low_two)
        hidden = contract(w_up, whole_two, 0, 0) + up_bias[layer][:, None]
        active = jax.nn.gelu(hidden, approximate=False).astype(jnp.bfloat16)
        residual = middle + scatter_tokens(contract(w_down, active, 1, 0)) + bias[5][:, None]
        saved.append(
            (
                w_qkv,
                w_out,
                w_up,
                w_down,
                whole_one,
                normed_one,
                inverse_one,
                queries,
                key_rows,
                value_rows,
                heads,
                low_heads,
                logsum,
                whole_two,
                normed_two,
                inverse_two,
                hidden,
                active,
            )
        )
    activations = tokens_to_features(residual.astype(jnp.bfloat16))

    def shared(grad):
        return scatter_blocks(
            grad.reshape(wide_count, -1, grad.shape[1]), "wide", jnp.bfloat16
        )

    gradient = features_to_tokens(cotangent).astype(jnp.float32)
    results = []
    for layer in reversed(range(layers)):
        (
            w_qkv,
            w_out,
            w_up,
            w_down,
            whole_one,
            normed_one,
            inverse_one,
            queries,
            key_rows,
            value_rows,
            heads,
            low_heads,
            logsum,
            whole_two,
            normed_two,
            inverse_two,
            hidden,
            active,
        ) = saved[layer]
        whole_grad = gather_tokens(gradient.astype(jnp.bfloat16))
        down_shift = jnp.sum(gradient, 1)
        act_grad = contract(w_down, whole_grad, 0, 0)
        hidden_grad = (act_grad * gelu_slope(hidden)).astype(jnp.bfloat16)
        two_grad = scatter_tokens(contract(w_up, hidden_grad, 1, 0))
        hidden_sum = jnp.sum(hidden_grad.astype(jnp.float32), 1)
        down_share = shared(contract(whole_grad, active, 1, 1))
        up_share = shared(contract(whole_two, hidden_grad, 1, 1))
        back_two, gain_two, shift_two = norm_backward(
            two_grad, normed_two, inverse_two, gain_all[layer, 1]
        )
        gradient = gradient + back_two
        if layer == layers - 1:
            activations, gradient = lax.optimization_barrier((activations, gradient))
        out_shift = jnp.sum(gradient, 1)
        whole_grad = gather_tokens(gradient.astype(jnp.bfloat16))
        heads_grad = head_blocks(contract(whole_grad, w_out, 0, 0).astype(jnp.bfloat16))
        out_share = shared(contract(whole_grad, low_heads, 1, 0))
        inner_sums = jnp.sum(heads_grad.astype(jnp.float32) * heads, -1).transpose(0, 2, 1)
        (key_grad, value_grad), query_grad = attend_backward(
            queries, heads_grad, inner_sums, logsum, key_rows, value_rows, bounds, spans
        )
        kv_grad = jnp.concatenate(
            [
                (key_grad * HEAD_DIM**-0.5).reshape(-1, width_here),
                value_grad.reshape(-1, width_here),
            ],
            axis=1,
        )
        from_upper = along_path(kv_grad[:tokens].astype(jnp.bfloat16), -1)
        from_lower = along_path(kv_grad[2 * tokens :].astype(jnp.bfloat16), 1)
        kv_grad = (
            kv_grad[tokens : 2 * tokens]
            + from_upper.astype(jnp.float32)
            + from_lower.astype(jnp.float32)
        )
        query_grad = (query_grad * HEAD_DIM**-0.5).reshape(tokens, width_here)
        qkv_grad = jnp.concatenate([query_grad, kv_grad], axis=1).astype(jnp.bfloat16)
        one_grad = scatter_tokens(contract(w_qkv, qkv_grad, 1, 1))
        qkv_share = shared(contract(whole_one, qkv_grad, 1, 0))
        head_sums = jnp.sum(qkv_grad.astype(jnp.float32), 0)
        back_one, gain_one, shift_one = norm_backward(
            one_grad, normed_one, inverse_one, gain_all[layer, 0]
        )
        gradient = gradient + back_one

        def placed(sums):
            return lax.dynamic_update_slice_in_dim(
                jnp.zeros((d_model,), jnp.float32), sums, narrow * width_here, 0
            )

        rows = jnp.stack(
            [
                gain_one,
                gain_two,
                shift_one,
                placed(head_sums[:width_here]),
                placed(head_sums[2 * width_here :]),
                out_shift,
                shift_two,
                down_shift,
            ]
        )
        up_sums = lax.dynamic_update_slice_in_dim(
            jnp.zeros((4, hidden_here), jnp.float32), hidden_sum[None], narrow, 0
        )
        small = jnp.concatenate(
            [
                rows.reshape(8, devices, -1).transpose(1, 0, 2).reshape(devices, -1),
                up_sums.reshape(devices, -1),
            ],
            axis=1,
        )
        results.append((qkv_share, out_share, up_share, down_share, small))
    results = results[::-1]
    grad_input = tokens_to_features(gradient.astype(jnp.bfloat16)).astype(jnp.float32)
    small = jnp.stack([entry[4] for entry in results], axis=1)
    small = scatter_blocks(
        small.reshape((4, wide_count) + small.shape[1:]), "narrow", jnp.float32
    )
    small = scatter_blocks(small, "wide", jnp.float32)
    row_part = small[:, : 8 * gains.shape[2]].reshape(layers, 8, -1)
    qkv, out, up, down = (jnp.stack([entry[i] for entry in results]) for i in range(4))
    return (
        activations,
        grad_input,
        qkv.reshape(layers, -1, 3, width_here).transpose(0, 2, 1, 3),
        out.transpose(0, 2, 1),
        up,
        down.transpose(0, 2, 1),
        row_part[:, :2],
        row_part[:, 2:],
        small[:, 8 * gains.shape[2] :],
    )


def solution(mesh):
    in_specs = (
        P("narrow", "wide"),
        P(None, "wide"),
        P(None, None, "wide", "narrow"),
        P(None, "narrow", "wide"),
        P(None, "wide", "narrow"),
        P(None, "narrow", "wide"),
        P(None, None, ("narrow", "wide")),
        P(None, None, ("narrow", "wide")),
        P(None, ("narrow", "wide")),
        P("narrow", "wide"),
    )
    out_specs = (
        P("narrow", "wide"),
        P("narrow", "wide"),
        P(None, None, "wide", "narrow"),
        P(None, "narrow", "wide"),
        P(None, "wide", "narrow"),
        P(None, "narrow", "wide"),
        P(None, None, ("narrow", "wide")),
        P(None, None, ("narrow", "wide")),
        P(None, ("narrow", "wide")),
    )
    return jax.shard_map(local, mesh=mesh, in_specs=in_specs, out_specs=out_specs, check_vma=False)
```

time: 2300 us -> 1680 us (0.73)
  blocking collectives: 481 us -> 0 us
  matrix products: 721 us -> 256 us
  loops' own time: 1.3 us -> 296 us
  waiting for transfers between devices: 600 us -> 318 us
  starting transfers between devices: 38.9 us -> 295 us
  local copies, waits for them, and re-layouts: 106 us -> 345 us
  other arithmetic: 316 us -> 148 us
    all_gather x8 -> x0, blocking collectives: 330 us -> none  [the longest x2 126 us: local(): lax.all_gather(out_weight[layer_idx], 'wide', axis=1, tiled=True)]
    dot_general x50 -> x56, matrix products: 539 us -> 213 us  [the longest x26 81.4 us: contract(): lax.dot_general(left, right, (((left_dim,), (right_dim,)), ((), ())), pre...]
    another operation x4 -> x16, loops' own time: 1.3 us -> 296 us  [the longest x12 171 us: by_window(): lax.switch(choice, [functools.partial(lambda size, *given: branch(size, j...]
    ppermute x8 -> x103, starting transfers between devices: 27.8 us -> 295 us  [the longest x46 233 us: swapped(): return lax.ppermute(value, axis, [(i, i ^ mask) for i in range(count)])]
    ppermute x8 -> x103, waiting for transfers between devices: 93.1 us -> 318 us  [the longest x46 134 us: swapped(): return lax.ppermute(value, axis, [(i, i ^ mask) for i in range(count)])]
    reduce_scatter x12 -> x0, waiting for transfers between devices: 218 us -> none  [the longest x4 126 us: input_total(): lax.psum_scatter(partial_sum.astype(jnp.bfloat16), 'narrow', scatter_dime...]
    all_gather x12 -> x0, waiting for transfers between devices: 156 us -> none  [the longest x4 73.5 us: branch_spread(): lax.all_gather(gradient.astype(jnp.bfloat16), 'narrow', axis=1, tiled=True)]
    dynamic_update_slice x0 -> x36, local copies, waits for them, and re-layouts: none -> 143 us  [the longest x6 66 us: branch(): lax.dynamic_update_slice_in_dim(key_grad, key_part, first, 0)]
  transfers between devices with their start and end apart: 36 -> 103, of which waited for: 21 -> 55; matrix products, arithmetic and copies ran while one was open for 20% -> 21% of each run, Pallas kernels for 0% -> 0%
where the time goes in v1:
time: 1680 us; the launch traced here: 1660 us
  local copies, waits for them, and re-layouts  345 us (21%)
  waiting for transfers between devices  318 us (19%)
  loops' own time  296 us (18%)
  starting transfers between devices  295 us (18%)
  matrix products  256 us (15%)
  other arithmetic  148 us (9%)
    ppermute x46, starting transfers between devices, swapped(): return lax.ppermute(value, axis, [(i, i ^ mask) for i in range(count)])  233 us
    another operation x12, loops' own time, by_window(): lax.switch(choice, [functools.partial(lambda size, *given: branch(size, j...  171 us
    ppermute x46, waiting for transfers between devices, swapped(): return lax.ppermute(value, axis, [(i, i ^ mask) for i in range(count)])  134 us
    ppermute x32, waiting for transfers between devices, partner(): return lax.ppermute(value, 'narrow', [(i, i ^ mask) for i in range(4)])  117 us
    dot_general x26, matrix products, contract(): lax.dot_general(left, right, (((left_dim,), (right_dim,)), ((), ())), pre...  81.4 us
    another operation x2, loops' own time, attend_forward(): return lax.map(one_block, (queries, bounds[0], bounds[1], spans))  69.4 us
    dynamic_update_slice x6, local copies, waits for them, and re-layouts, branch(): lax.dynamic_update_slice_in_dim(key_grad, key_part, first, 0)  66 us
    another operation x2, loops' own time, attend_backward(): lax.scan(one_block, (zeros, zeros), (queries, grads, inner_sums, logsums,...  55.9 us
  transfers between devices with their start and end apart: 103, of which 55 were waited for; matrix products, arithmetic and copies ran while one was open for 21% of the time, Pallas kernels for 0%

profile of v1, /device:TPU:0, one launch (start us, length us, event | category | flops | bytes accessed | tf_op | source)
XLA Modules:
  0.0 1661.9 jit_solution(12187322080983187948)
XLA Ops:
  95.5 15.6 collective-permute-done.6
  114.6 19.8 %collective-permute-done.19 = bf16[1536,384]{1,0:T(8,128)(2,1)} collective-permute-done((bf16[1536,384]{1,0:T(8,128)(2,1)S(1)}, bf16[1536,384]{1,0:T(8,128)(2,1)}, u32[]{:S(2)}, u32[]{:S(2)}) %collective-permute-start.19) | collective-permute-done | bytes 1179680 | tf_op jit(solution)/shard_map/ppermute | solution.py:130
  148.4 131.4 %while.60 = (s32[]{:T(128)}, f32[3,512,3,64]{1,3,2,0:T(8,128)}, f32[3,3,512]{2,1,0:T(4,128)}, s32[3,2]{0,1:T(2,128)}, bf16[3,512,3,64]{1,3,2,0:T(8,128)(2,1)}, /...) while((s32[]{:T(128)}, f32[3,512,3,64]{1,3,2,0:T(8,128)}, ...), condition=%wide.region_21.22_spmd, body=%wide.region_2.21_spmd.sunk | while | flops 1903954944 | bytes 149295024 | solution.py:70
  154.9 26.4 %conditional.8 = (f32[1,512,3,64]{1,3,2,0:T(8,128)}, f32[1,3,512]{2,1,0:T(4,128)S(1)}) conditional(s32[]{:T(128)} %clamp.28, (s32[]{:T(128)}, bf16[4608,3,64]{0,2,1:T(8,128)(2,1)}, s32[512]{0:T(512)S(1)}, s32[512]{0:T(512)S(1)}, bf16[4608,3,64]{0,2,1:T(8,128)(2,1)S(1)}, ...), branch_computations={%region_3.5_spmd, %region_6.8_spmd, %region_9.11_spmd, %region_12.... | conditional | flops 1903954944 | bytes 148092016 | solution.py:30
  195.9 26.4 %conditional.8 = (f32[1,512,3,64]{1,3,2,0:T(8,128)}, f32[1,3,512]{2,1,0:T(4,128)S(1)}) conditional(s32[]{:T(128)} %clamp.28, (s32[]{:T(128)}, bf16[4608,3,64]{0,2,1:T(8,128)(2,1)}, s32[512]{0:T(512)S(1)}, s32[512]{0:T(512)S(1)}, bf16[4608,3,64]{0,2,1:T(8,128)(2,1)S(1)}, ...), branch_computations={%region_3.5_spmd, %region_6.8_spmd, %region_9.11_spmd, %region_12.... | conditional | flops 1903954944 | bytes 148092016 | solution.py:30
  236.7 26.3 %conditional.8 = (f32[1,512,3,64]{1,3,2,0:T(8,128)}, f32[1,3,512]{2,1,0:T(4,128)S(1)}) conditional(s32[]{:T(128)} %clamp.28, (s32[]{:T(128)}, bf16[4608,3,64]{0,2,1:T(8,128)(2,1)}, s32[512]{0:T(512)S(1)}, s32[512]{0:T(512)S(1)}, bf16[4608,3,64]{0,2,1:T(8,128)(2,1)S(1)}, ...), branch_computations={%region_3.5_spmd, %region_6.8_spmd, %region_9.11_spmd, %region_12.... | conditional | flops 1903954944 | bytes 148092016 | solution.py:30
  331.6 14.3 fusion.368
  430.9 18.6 %collective-permute-done.28 = bf16[2,2,96,1728]{3,2,0,1:T(8,128)(2,1)S(1)} collective-permute-done((bf16[2,2,96,1728]{3,2,0,1:T(8,128)(2,1)S(1)}, bf16[2,2,96,1728]{3,2,0,1:T(8,128)(2,1)S(1)}, u32[]{:S(2)}, u32[]{:S(2)}) %collective-permute-start.28) | collective-permute-done | bytes 1327136 | tf_op jit(solution)/shard_map/ppermute | solution.py:175
  455.5 16.9 %collective-permute-done.35 = bf16[1536,384]{1,0:T(8,128)(2,1)S(1)} collective-permute-done((bf16[1536,384]{1,0:T(8,128)(2,1)S(1)}, bf16[1536,384]{1,0:T(8,128)(2,1)S(1)}, u32[]{:S(2)}, u32[]{:S(2)}) %collective-permute-start.35) | collective-permute-done | bytes 1179680 | tf_op jit(solution)/shard_map/ppermute | solution.py:130
  486.2 128.1 %while.61 = (s32[]{:T(128)}, f32[3,512,3,64]{1,3,2,0:T(8,128)}, f32[3,3,512]{2,1,0:T(4,128)}, s32[3,2]{0,1:T(2,128)}, bf16[3,512,3,64]{1,3,2,0:T(8,128)(2,1)}, /...) while((s32[]{:T(128)}, f32[3,512,3,64]{1,3,2,0:T(8,128)}, ...), condition=%wide.region_45.46_spmd, body=%wide.region_26.45_spmd.sunk | while | flops 1903954944 | bytes 149295024 | solution.py:70
  492.8 26.4 %conditional.9 = (f32[1,512,3,64]{1,3,2,0:T(8,128)}, f32[1,3,512]{2,1,0:T(4,128)S(1)}) conditional(s32[]{:T(128)} %clamp.29, (s32[]{:T(128)}, bf16[4608,3,64]{0,2,1:T(8,128)(2,1)}, s32[512]{0:T(512)S(1)}, s32[512]{0:T(512)S(1)}, bf16[4608,3,64]{0,2,1:T(8,128)(2,1)S(1)}, ...), branch_computations={%region_27.29_spmd, %region_30.32_spmd, %region_33.35_spmd, %regio... | conditional | flops 1903954944 | bytes 148092016 | solution.py:30
  533.5 26.3 %conditional.9 = (f32[1,512,3,64]{1,3,2,0:T(8,128)}, f32[1,3,512]{2,1,0:T(4,128)S(1)}) conditional(s32[]{:T(128)} %clamp.29, (s32[]{:T(128)}, bf16[4608,3,64]{0,2,1:T(8,128)(2,1)}, s32[512]{0:T(512)S(1)}, s32[512]{0:T(512)S(1)}, bf16[4608,3,64]{0,2,1:T(8,128)(2,1)S(1)}, ...), branch_computations={%region_27.29_spmd, %region_30.32_spmd, %region_33.35_spmd, %regio... | conditional | flops 1903954944 | bytes 148092016 | solution.py:30
  574.3 26.4 %conditional.9 = (f32[1,512,3,64]{1,3,2,0:T(8,128)}, f32[1,3,512]{2,1,0:T(4,128)S(1)}) conditional(s32[]{:T(128)} %clamp.29, (s32[]{:T(128)}, bf16[4608,3,64]{0,2,1:T(8,128)(2,1)}, s32[512]{0:T(512)S(1)}, s32[512]{0:T(512)S(1)}, bf16[4608,3,64]{0,2,1:T(8,128)(2,1)S(1)}, ...), branch_computations={%region_27.29_spmd, %region_30.32_spmd, %region_33.35_spmd, %regio... | conditional | flops 1903954944 | bytes 148092016 | solution.py:30
  788.1 22.0 %collective-permute-start.91 = (bf16[1,96,768]{2,1,0:T(8,128)(2,1)S(1)}, bf16[1,96,768]{2,1,0:T(8,128)(2,1)S(1)}, u32[]{:S(2)}, u32[]{:S(2)}) collective-permute-start(bf16[1,96,768]{2,1,0:T(8,128)(2,1)S(1)} %fusion.529), channel_id=1, source_target_pairs={{0,16},{4,20},{8,24},{12,28},{16,0},{20,4},{24,8},{28,12},{1,17},{... | collective-permute-start | bytes 442376 | tf_op jit(solution)/shard_map/ppermute | solution.py:175
  828.4 213.9 %while.62 = (s32[]{:T(128)}, f32[4608,3,64]{0,2,1:T(8,128)S(1)}, f32[4608,3,64]{0,2,1:T(8,128)}, f32[3,512,3,64]{1,3,2,0:T(8,128)}, s32[3,2]{0,1:T(2,128)}, /*in...) while((s32[]{:T(128)}, f32[4608,3,64]{0,2,1:T(8,128)S(1)}, ...), condition=%wide.region_58.59_spmd, body=%wide.region_51.58_spmd.sunk | while | flops 4609479168 | bytes 165477648 | solution.py:115
  837.7 54.6 %conditional.10 = (f32[4608,3,64]{0,2,1:T(8,128)S(1)}, f32[4608,3,64]{0,2,1:T(8,128)}, f32[1,512,3,64]{1,3,2,0:T(8,128)}) conditional(s32[]{:T(128)} %clamp.30, (s32[]{:T(128)}, s32[512]{0:T(512)S(1)}, s32[512]{0:T(512)S(1)}, bf16[4608,3,64]{0,2,1:T(8,128)(2,1)}, bf16[512,3,64]{0,2,1:T(8,128)(2,1)}, ...), branch_computations={%region_52.52_spmd, %region_53.53_spmd, %region_54.54_spmd, %regio... | conditional | flops 4609479168 | bytes 163858592 | solution.py:30
  906.5 54.6 %conditional.10 = (f32[4608,3,64]{0,2,1:T(8,128)S(1)}, f32[4608,3,64]{0,2,1:T(8,128)}, f32[1,512,3,64]{1,3,2,0:T(8,128)}) conditional(s32[]{:T(128)} %clamp.30, (s32[]{:T(128)}, s32[512]{0:T(512)S(1)}, s32[512]{0:T(512)S(1)}, bf16[4608,3,64]{0,2,1:T(8,128)(2,1)}, bf16[512,3,64]{0,2,1:T(8,128)(2,1)}, ...), branch_computations={%region_52.52_spmd, %region_53.53_spmd, %region_54.54_spmd, %regio... | conditional | flops 4609479168 | bytes 163858592 | solution.py:30
  975.6 54.6 %conditional.10 = (f32[4608,3,64]{0,2,1:T(8,128)S(1)}, f32[4608,3,64]{0,2,1:T(8,128)}, f32[1,512,3,64]{1,3,2,0:T(8,128)}) conditional(s32[]{:T(128)} %clamp.30, (s32[]{:T(128)}, s32[512]{0:T(512)S(1)}, s32[512]{0:T(512)S(1)}, bf16[4608,3,64]{0,2,1:T(8,128)(2,1)}, bf16[512,3,64]{0,2,1:T(8,128)(2,1)}, ...), branch_computations={%region_52.52_spmd, %region_53.53_spmd, %region_54.54_spmd, %regio... | conditional | flops 4609479168 | bytes 163858592 | solution.py:30
  1044.8 43.3 %collective-permute-start.83 = (bf16[4,96,192]{2,1,0:T(8,128)(2,1)S(1)}, bf16[4,96,192]{2,1,0:T(8,128)(2,1)S(1)}, u32[]{:S(2)}, u32[]{:S(2)}) collective-permute-start(bf16[4,96,192]{2,1,0:T(8,128)(2,1)S(1)} %fusion.525), channel_id=1, source_target_pairs={{0,4},{4,0},{8,12},{12,8},{16,20},{20,16},{24,28},{28,24},{1,5},{5... | collective-permute-start | bytes 442376 | tf_op jit(solution)/shard_map/ppermute | solution.py:175
  1279.5 215.5 %while.63 = (s32[]{:T(128)}, f32[4608,3,64]{0,2,1:T(8,128)S(1)}, f32[4608,3,64]{0,2,1:T(8,128)}, f32[3,512,3,64]{1,3,2,0:T(8,128)}, s32[3,2]{0,1:T(2,128)}, /*in...) while((s32[]{:T(128)}, f32[4608,3,64]{0,2,1:T(8,128)S(1)}, ...), condition=%wide.region_71.72_spmd, body=%wide.region_64.71_spmd.sunk | while | flops 4609479168 | bytes 165477648 | solution.py:115
  1288.8 54.5 %conditional.11 = (f32[4608,3,64]{0,2,1:T(8,128)S(1)}, f32[4608,3,64]{0,2,1:T(8,128)}, f32[1,512,3,64]{1,3,2,0:T(8,128)}) conditional(s32[]{:T(128)} %clamp.31, (s32[]{:T(128)}, s32[512]{0:T(512)S(1)}, s32[512]{0:T(512)S(1)}, bf16[4608,3,64]{0,2,1:T(8,128)(2,1)}, bf16[512,3,64]{0,2,1:T(8,128)(2,1)}, ...), branch_computations={%region_65.65_spmd, %region_66.66_spmd, %region_67.67_spmd, %regio... | conditional | flops 4609479168 | bytes 163858592 | solution.py:30
  1357.7 54.7 %conditional.11 = (f32[4608,3,64]{0,2,1:T(8,128)S(1)}, f32[4608,3,64]{0,2,1:T(8,128)}, f32[1,512,3,64]{1,3,2,0:T(8,128)}) conditional(s32[]{:T(128)} %clamp.31, (s32[]{:T(128)}, s32[512]{0:T(512)S(1)}, s32[512]{0:T(512)S(1)}, bf16[4608,3,64]{0,2,1:T(8,128)(2,1)}, bf16[512,3,64]{0,2,1:T(8,128)(2,1)}, ...), branch_computations={%region_65.65_spmd, %region_66.66_spmd, %region_67.67_spmd, %regio... | conditional | flops 4609479168 | bytes 163858592 | solution.py:30
  1427.0 54.7 %conditional.11 = (f32[4608,3,64]{0,2,1:T(8,128)S(1)}, f32[4608,3,64]{0,2,1:T(8,128)}, f32[1,512,3,64]{1,3,2,0:T(8,128)}) conditional(s32[]{:T(128)} %clamp.31, (s32[]{:T(128)}, s32[512]{0:T(512)S(1)}, s32[512]{0:T(512)S(1)}, bf16[4608,3,64]{0,2,1:T(8,128)(2,1)}, bf16[512,3,64]{0,2,1:T(8,128)(2,1)}, ...), branch_computations={%region_65.65_spmd, %region_66.66_spmd, %region_67.67_spmd, %regio... | conditional | flops 4609479168 | bytes 163858592 | solution.py:30
  1497.7 42.7 %collective-permute-start.80 = (bf16[4,96,192]{2,1,0:T(8,128)(2,1)S(1)}, bf16[4,96,192]{2,1,0:T(8,128)(2,1)S(1)}, u32[]{:S(2)}, u32[]{:S(2)}) collective-permute-start(bf16[4,96,192]{2,1,0:T(8,128)(2,1)S(1)} %fusion.524), channel_id=1, source_target_pairs={{0,4},{4,0},{8,12},{12,8},{16,20},{20,16},{24,28},{28,24},{1,5},{5... | collective-permute-start | bytes 442376 | tf_op jit(solution)/shard_map/ppermute | solution.py:175
  (1169 shorter events, 1168.1 us)
Async XLA Ops:
  10.3 30.2 %collective-permute-start.15 = (bf16[96,576]{0,1:T(8,128)(2,1)S(1)}, bf16[96,576]{0,1:T(8,128)(2,1)S(1)}, u32[]{:S(2)}, u32[]{:S(2)}) collective-permute-start(bf16[96,576]{0,1:T(8,128)(2,1)S(1)} %bitcast.1643), channel_id=1, source_target_pairs={{0,16},{4,20},{8,24},{12,28},{16,0},{20,4},{24,8},{28,12},{1,17},{... | collective-permute-start | bytes 331784 | tf_op jit(solution)/shard_map/ppermute | solution.py:175
  15.3 34.3 %collective-permute-start.4 = (bf16[96,1728]{1,0:T(8,128)(2,1)S(1)}, bf16[96,1728]{1,0:T(8,128)(2,1)}, u32[]{:S(2)}, u32[]{:S(2)}) collective-permute-start(bf16[96,1728]{1,0:T(8,128)(2,1)S(1)} %pad_maximum_fusion.64), channel_id=1, source_target_pairs={{0,16},{4,20},{8,24},{12,28},{16,0},{20,4},{24,8},{28,12},{1,17},{... | collective-permute-start | bytes 995336 | tf_op jit(solution)/shard_map/ppermute | solution.py:175
  77.6 33.4 %collective-permute-start.6 = (bf16[2,2,96,1728]{3,2,0,1:T(8,128)(2,1)}, bf16[2,2,96,1728]{3,2,0,1:T(8,128)(2,1)}, u32[]{:S(2)}, u32[]{:S(2)}) collective-permute-start(bf16[2,2,96,1728]{3,2,0,1:T(8,128)(2,1)} %pad_maximum_fusion.31), channel_id=1, source_target_pairs={{0,4},{4,0},{8,12},{12,8},{16,20},{20,16},{24,28},{28,24},{1,5},{5... | collective-permute-start | bytes 3981320 | tf_op jit(solution)/shard_map/ppermute | solution.py:175
  84.4 49.9 %collective-permute-start.19 = (bf16[1536,384]{1,0:T(8,128)(2,1)S(1)}, bf16[1536,384]{1,0:T(8,128)(2,1)}, u32[]{:S(2)}, u32[]{:S(2)}) collective-permute-start(bf16[1536,384]{1,0:T(8,128)(2,1)S(1)} %fusion.398), channel_id=1, source_target_pairs={{4,0},{12,4},{8,12},{16,8},{20,16},{28,20},{24,28},{5,1},{13,5},{9... | collective-permute-start | bytes 3538952 | tf_op jit(solution)/shard_map/ppermute | solution.py:130
  85.7 48.6 %collective-permute-start.18 = (bf16[1536,384]{1,0:T(8,128)(2,1)S(1)}, bf16[1536,384]{1,0:T(8,128)(2,1)}, u32[]{:S(2)}, u32[]{:S(2)}) collective-permute-start(bf16[1536,384]{1,0:T(8,128)(2,1)S(1)} %fusion.398), channel_id=1, source_target_pairs={{0,4},{4,12},{12,8},{8,16},{16,20},{20,28},{28,24},{1,5},{5,13},{1... | collective-permute-start | bytes 3538952 | tf_op jit(solution)/shard_map/ppermute | solution.py:130
  408.9 40.6 %collective-permute-start.28 = (bf16[2,2,96,1728]{3,2,0,1:T(8,128)(2,1)S(1)}, bf16[2,2,96,1728]{3,2,0,1:T(8,128)(2,1)S(1)}, u32[]{:S(2)}, u32[]{:S(2)}) collective-permute-start(bf16[2,2,96,1728]{3,2,0,1:T(8,128)(2,1)S(1)} %pad_maximum_fusion.32), channel_id=1, source_target_pairs={{0,4},{4,0},{8,12},{12,8},{16,20},{20,16},{24,28},{28,24},{1,5},{5... | collective-permute-start | bytes 3981320 | tf_op jit(solution)/shard_map/ppermute | solution.py:175
  423.9 48.5 %collective-permute-start.35 = (bf16[1536,384]{1,0:T(8,128)(2,1)S(1)}, bf16[1536,384]{1,0:T(8,128)(2,1)S(1)}, u32[]{:S(2)}, u32[]{:S(2)}) collective-permute-start(bf16[1536,384]{1,0:T(8,128)(2,1)S(1)} %fusion.399), channel_id=1, source_target_pairs={{4,0},{12,4},{8,12},{16,8},{20,16},{28,20},{24,28},{5,1},{13,5},{9... | collective-permute-start | bytes 3538952 | tf_op jit(solution)/shard_map/ppermute | solution.py:130
  425.2 47.2 %collective-permute-start.34 = (bf16[1536,384]{1,0:T(8,128)(2,1)S(1)}, bf16[1536,384]{1,0:T(8,128)(2,1)}, u32[]{:S(2)}, u32[]{:S(2)}) collective-permute-start(bf16[1536,384]{1,0:T(8,128)(2,1)S(1)} %fusion.399), channel_id=1, source_target_pairs={{0,4},{4,12},{12,8},{8,16},{16,20},{20,28},{28,24},{1,5},{5,13},{1... | collective-permute-start | bytes 3538952 | tf_op jit(solution)/shard_map/ppermute | solution.py:130
  624.1 25.2 %collective-permute-start.37 = (bf16[768,384]{1,0:T(8,128)(2,1)S(1)}, bf16[768,384]{1,0:T(8,128)(2,1)}, u32[]{:S(2)}, u32[]{:S(2)}) collective-permute-start(bf16[768,384]{1,0:T(8,128)(2,1)S(1)} %fusion.477), channel_id=1, source_target_pairs={{0,2},{1,3},{2,0},{3,1},{4,6},{5,7},{6,4},{7,5},{8,10},{9,11},{10,... | collective-permute-start | bytes 1769480 | tf_op jit(solution)/shard_map/ppermute | solution.py:141
  651.3 23.8 %collective-permute-start.38 = (bf16[768,384]{1,0:T(8,128)(2,1)S(1)}, bf16[768,384]{1,0:T(8,128)(2,1)S(1)}, u32[]{:S(2)}, u32[]{:S(2)}) collective-permute-start(bf16[768,384]{1,0:T(8,128)(2,1)S(1)} %add_convert_fusion), channel_id=1, source_target_pairs={{0,2},{1,3},{2,0},{3,1},{4,6},{5,7},{6,4},{7,5},{8,10},{9,11},{10,... | collective-permute-start | bytes 1769480 | tf_op jit(solution)/shard_map/ppermute | solution.py:141
  725.5 48.4 %collective-permute-start.95 = (bf16[4,96,768]{2,1,0:T(8,128)(2,1)}, bf16[4,96,768]{2,1,0:T(8,128)(2,1)S(1)}, u32[]{:S(2)}, u32[]{:S(2)}) collective-permute-start(bf16[4,96,768]{2,1,0:T(8,128)(2,1)} %fusion.486), channel_id=1, source_target_pairs={{0,4},{4,0},{8,12},{12,8},{16,20},{20,16},{24,28},{28,24},{1,5},{5... | collective-permute-start | bytes 1769480 | tf_op jit(solution)/shard_map/ppermute | solution.py:175
  761.7 26.2 %collective-permute-start.90 = (bf16[2,96,768]{2,1,0:T(8,128)(2,1)S(1)}, bf16[2,96,768]{2,1,0:T(8,128)(2,1)S(1)}, u32[]{:S(2)}, u32[]{:S(2)}) collective-permute-start(bf16[2,96,768]{2,1,0:T(8,128)(2,1)S(1)} %fusion.519), channel_id=1, source_target_pairs={{0,8},{4,12},{8,0},{12,4},{16,24},{20,28},{24,16},{28,20},{1,9},{5... | collective-permute-start | bytes 884744 | tf_op jit(solution)/shard_map/ppermute | solution.py:175
  774.1 35.9 %collective-permute-start.96 = (bf16[2,96,768]{2,1,0:T(8,128)(2,1)S(1)}, bf16[2,96,768]{2,1,0:T(8,128)(2,1)S(1)}, u32[]{:S(2)}, u32[]{:S(2)}) collective-permute-start(bf16[2,96,768]{2,1,0:T(8,128)(2,1)S(1)} %fusion.521), channel_id=1, source_target_pairs={{0,8},{4,12},{8,0},{12,4},{16,24},{20,28},{24,16},{28,20},{1,9},{5... | collective-permute-start | bytes 884744 | tf_op jit(solution)/shard_map/ppermute | solution.py:175
  787.8 29.1 %collective-permute-start.55 = (bf16[2,768,384]{2,1,0:T(8,128)(2,1)S(1)}, bf16[2,768,384]{2,1,0:T(8,128)(2,1)S(1)}, u32[]{:S(2)}, u32[]{:S(2)}) collective-permute-start(bf16[2,768,384]{2,1,0:T(8,128)(2,1)S(1)} %pad_maximum_fusion.40), channel_id=1, source_target_pairs={{0,1},{1,0},{2,3},{3,2},{4,5},{5,4},{6,7},{7,6},{8,9},{9,8},{10,11... | collective-permute-start | bytes 3538952 | tf_op jit(solution)/shard_map/ppermute | solution.py:141
  788.1 28.1 %collective-permute-start.91 = (bf16[1,96,768]{2,1,0:T(8,128)(2,1)S(1)}, bf16[1,96,768]{2,1,0:T(8,128)(2,1)S(1)}, u32[]{:S(2)}, u32[]{:S(2)}) collective-permute-start(bf16[1,96,768]{2,1,0:T(8,128)(2,1)S(1)} %fusion.529), channel_id=1, source_target_pairs={{0,16},{4,20},{8,24},{12,28},{16,0},{20,4},{24,8},{28,12},{1,17},{... | collective-permute-start | bytes 442376 | tf_op jit(solution)/shard_map/ppermute | solution.py:175
  810.9 330.8 %collective-permute-start.97 = (bf16[1,96,768]{2,1,0:T(8,128)(2,1)}, bf16[1,96,768]{2,1,0:T(8,128)(2,1)}, u32[]{:S(2)}, u32[]{:S(2)}) collective-permute-start(bf16[1,96,768]{2,1,0:T(8,128)(2,1)} %fusion.531), channel_id=1, source_target_pairs={{0,16},{4,20},{8,24},{12,28},{16,0},{20,4},{24,8},{28,12},{1,17},{... | collective-permute-start | bytes 442376 | tf_op jit(solution)/shard_map/ppermute | solution.py:175
  1044.8 55.5 %collective-permute-start.83 = (bf16[4,96,192]{2,1,0:T(8,128)(2,1)S(1)}, bf16[4,96,192]{2,1,0:T(8,128)(2,1)S(1)}, u32[]{:S(2)}, u32[]{:S(2)}) collective-permute-start(bf16[4,96,192]{2,1,0:T(8,128)(2,1)S(1)} %fusion.525), channel_id=1, source_target_pairs={{0,4},{4,0},{8,12},{12,8},{16,20},{20,16},{24,28},{28,24},{1,5},{5... | collective-permute-start | bytes 442376 | tf_op jit(solution)/shard_map/ppermute | solution.py:175
  1093.4 29.9 %collective-permute-start.56 = (bf16[1536,384]{0,1:T(8,128)(2,1)}, bf16[1536,384]{0,1:T(8,128)(2,1)}, u32[]{:S(2)}, u32[]{:S(2)}) collective-permute-start(bf16[1536,384]{0,1:T(8,128)(2,1)} %get-tuple-element.1644), channel_id=1, source_target_pairs={{4,0},{12,4},{8,12},{16,8},{20,16},{28,20},{24,28},{5,1},{13,5},{9... | collective-permute-start | bytes 3538952 | tf_op jit(solution)/shard_map/ppermute | solution.py:130
  1094.7 29.8 %collective-permute-start.57 = (bf16[1536,384]{0,1:T(8,128)(2,1)}, bf16[1536,384]{0,1:T(8,128)(2,1)}, u32[]{:S(2)}, u32[]{:S(2)}) collective-permute-start(bf16[1536,384]{0,1:T(8,128)(2,1)} %get-tuple-element.1645), channel_id=1, source_target_pairs={{0,4},{4,12},{12,8},{8,16},{16,20},{20,28},{28,24},{1,5},{5,13},{1... | collective-permute-start | bytes 3538952 | tf_op jit(solution)/shard_map/ppermute | solution.py:130
  1130.3 23.2 %collective-permute-start.58 = (bf16[2,768,384]{2,1,0:T(8,128)(2,1)}, bf16[2,768,384]{2,1,0:T(8,128)(2,1)}, u32[]{:S(2)}, u32[]{:S(2)}) collective-permute-start(bf16[2,768,384]{2,1,0:T(8,128)(2,1)} %select_convert_fusion.2), channel_id=1, source_target_pairs={{0,1},{1,0},{2,3},{3,2},{4,5},{5,4},{6,7},{7,6},{8,9},{9,8},{10,11... | collective-permute-start | bytes 3538952 | tf_op jit(solution)/shard_map/ppermute | solution.py:141
  1497.7 54.9 %collective-permute-start.80 = (bf16[4,96,192]{2,1,0:T(8,128)(2,1)S(1)}, bf16[4,96,192]{2,1,0:T(8,128)(2,1)S(1)}, u32[]{:S(2)}, u32[]{:S(2)}) collective-permute-start(bf16[4,96,192]{2,1,0:T(8,128)(2,1)S(1)} %fusion.524), channel_id=1, source_target_pairs={{0,4},{4,0},{8,12},{12,8},{16,20},{20,16},{24,28},{28,24},{1,5},{5... | collective-permute-start | bytes 442376 | tf_op jit(solution)/shard_map/ppermute | solution.py:175
  1545.6 29.6 %collective-permute-start.66 = (bf16[1536,384]{0,1:T(8,128)(2,1)}, bf16[1536,384]{0,1:T(8,128)(2,1)}, u32[]{:S(2)}, u32[]{:S(2)}) collective-permute-start(bf16[1536,384]{0,1:T(8,128)(2,1)} %get-tuple-element.1642), channel_id=1, source_target_pairs={{4,0},{12,4},{8,12},{16,8},{20,16},{28,20},{24,28},{5,1},{13,5},{9... | collective-permute-start | bytes 3538952 | tf_op jit(solution)/shard_map/ppermute | solution.py:130
  1546.9 29.5 %collective-permute-start.67 = (bf16[1536,384]{0,1:T(8,128)(2,1)}, bf16[1536,384]{0,1:T(8,128)(2,1)}, u32[]{:S(2)}, u32[]{:S(2)}) collective-permute-start(bf16[1536,384]{0,1:T(8,128)(2,1)} %get-tuple-element.1643), channel_id=1, source_target_pairs={{0,4},{4,12},{12,8},{8,16},{16,20},{20,28},{28,24},{1,5},{5,13},{1... | collective-permute-start | bytes 3538952 | tf_op jit(solution)/shard_map/ppermute | solution.py:130
  1568.2 38.2 %collective-permute-start.82 = (bf16[1,96,192]{1,2,0:T(8,128)(2,1)S(1)}, bf16[1,96,192]{1,2,0:T(8,128)(2,1)S(1)}, u32[]{:S(2)}, u32[]{:S(2)}) collective-permute-start(bf16[1,96,192]{1,2,0:T(8,128)(2,1)S(1)} %fusion.536), channel_id=1, source_target_pairs={{0,16},{4,20},{8,24},{12,28},{16,0},{20,4},{24,8},{28,12},{1,17},{... | collective-permute-start | bytes 110600 | tf_op jit(solution)/shard_map/ppermute | solution.py:175
  (259 other events, 2567.5 us)

commit v2 on v1

--- a/solution.py
+++ b/solution.py
@@ -1,5 +1,3 @@
-import functools
-
 import jax
 import jax.numpy as jnp
 from jax import lax
@@ -18,25 +16,10 @@
     )
 
 
-def window_sizes(rows):
-    return [size for size in (1152, 1664, 2176, 2688, 3200) if size < rows] + [rows]
-
-
-def by_window(spans, rows, branch, operands):
-    sizes = window_sizes(rows)
-    first = spans[0] // 128 * 128
-    needed = spans[1] - first
-    choice = sum((needed > size).astype(jnp.int32) for size in sizes[:-1])
-    return lax.switch(
-        choice,
-        [
-            functools.partial(
-                lambda size, *given: branch(size, jnp.clip(first, 0, rows - size), *given), size
-            )
-            for size in sizes
-        ],
-        *operands,
-    )
+def windows(queries, key_rows):
+    blocks, rows = queries.shape[:2]
+    size = rows + 2 * (key_rows.shape[0] // 3)
+    return [slice(i * rows, i * rows + size) for i in range(blocks)]
 
 
 def masked_scores(query_block, key_rows, starts, ends, first):
@@ -48,75 +31,54 @@
     return jnp.where(inside[None], scores, MASKED)
 
 
-def attend_forward(queries, key_rows, value_rows, bounds, spans):
-    def one_block(data):
-        query_block, starts, ends, span = data
-
-        def branch(size, first, query_block, starts, ends):
-            keys = lax.dynamic_slice_in_dim(key_rows, first, size, 0)
-            values = lax.dynamic_slice_in_dim(value_rows, first, size, 0)
-            scores = masked_scores(query_block, keys, starts, ends, first)
-            peak = jnp.max(scores, -1, keepdims=True)
-            weights = jnp.exp(scores - peak)
-            total = jnp.sum(weights, -1, keepdims=True)
-            probabilities = (weights / total).astype(jnp.bfloat16)
-            mixed = jnp.einsum(
-                "hqk,khd->qhd", probabilities, values, preferred_element_type=jnp.float32
-            )
-            return mixed, (peak + jnp.log(total))[..., 0]
-
-        return by_window(span, key_rows.shape[0], branch, (query_block, starts, ends))
-
-    return lax.map(one_block, (queries, bounds[0], bounds[1], spans))
-
-
-def attend_backward(queries, grads, inner_sums, logsums, key_rows, value_rows, bounds, spans):
-    def one_block(carried, data):
-        query_block, grad_block, inner, logsum, starts, ends, span = data
-
-        def branch(size, first, key_grad, value_grad, query_block, grad_block, inner, logsum, starts, ends):
-            keys = lax.dynamic_slice_in_dim(key_rows, first, size, 0)
-            values = lax.dynamic_slice_in_dim(value_rows, first, size, 0)
-            scores = masked_scores(query_block, keys, starts, ends, first)
-            weights = jnp.exp(scores - logsum[..., None])
-            weight_grad = jnp.einsum(
-                "qhd,khd->hqk", grad_block, values, preferred_element_type=jnp.float32
-            )
-            score_grad = (weights * (weight_grad - inner[..., None])).astype(jnp.bfloat16)
-            query_grad = jnp.einsum(
-                "hqk,khd->qhd", score_grad, keys, preferred_element_type=jnp.float32
-            )
-            key_part = jnp.einsum(
-                "hqk,qhd->khd", score_grad, query_block, preferred_element_type=jnp.float32
-            )
-            value_part = jnp.einsum(
-                "hqk,qhd->khd",
-                weights.astype(jnp.bfloat16),
-                grad_block,
+def attend_forward(queries, key_rows, value_rows, bounds):
+    mixed, logsums = [], []
+    for i, window in enumerate(windows(queries, key_rows)):
+        scores = masked_scores(
+            queries[i], key_rows[window], bounds[0, i], bounds[1, i], window.start
+        )
+        peak = jnp.max(scores, -1, keepdims=True)
+        weights = jnp.exp(scores - peak)
+        total = jnp.sum(weights, -1, keepdims=True)
+        probabilities = (weights / total).astype(jnp.bfloat16)
+        mixed.append(
+            jnp.einsum(
+                "hqk,khd->qhd",
+                probabilities,
+                value_rows[window],
                 preferred_element_type=jnp.float32,
             )
-            key_part = key_part + lax.dynamic_slice_in_dim(key_grad, first, size, 0)
-            value_part = value_part + lax.dynamic_slice_in_dim(value_grad, first, size, 0)
-            return (
-                lax.dynamic_update_slice_in_dim(key_grad, key_part, first, 0),
-                lax.dynamic_update_slice_in_dim(value_grad, value_part, first, 0),
-                query_grad,
-            )
-
-        key_grad, value_grad, query_grad = by_window(
-            span,
-            key_rows.shape[0],
-            branch,
-            (*carried, query_block, grad_block, inner, logsum, starts, ends),
-        )
-        return (key_grad, value_grad), query_grad
-
-    zeros = jnp.zeros(key_rows.shape, jnp.float32)
-    return lax.scan(
-        one_block,
-        (zeros, zeros),
-        (queries, grads, inner_sums, logsums, bounds[0], bounds[1], spans),
-    )
+        )
+        logsums.append((peak + jnp.log(total))[..., 0])
+    return jnp.stack(mixed), logsums
+
+
+def attend_backward(queries, grads, inner_sums, logsums, key_rows, value_rows, bounds):
+    query_grads, key_grad, value_grad = [], 0.0, 0.0
+    for i, window in enumerate(windows(queries, key_rows)):
+        keys, values = key_rows[window], value_rows[window]
+        scores = masked_scores(queries[i], keys, bounds[0, i], bounds[1, i], window.start)
+        weights = jnp.exp(scores - logsums[i][..., None])
+        weight_grad = jnp.einsum(
+            "qhd,khd->hqk", grads[i], values, preferred_element_type=jnp.float32
+        )
+        score_grad = (weights * (weight_grad - inner_sums[i][..., None])).astype(jnp.bfloat16)
+        query_grads.append(
+            jnp.einsum("hqk,khd->qhd", score_grad, keys, preferred_element_type=jnp.float32)
+        )
+        key_part = jnp.einsum(
+            "hqk,qhd->khd", score_grad, queries[i], preferred_element_type=jnp.float32
+        )
+        value_part = jnp.einsum(
+            "hqk,qhd->khd",
+            weights.astype(jnp.bfloat16),
+            grads[i],
+            preferred_element_type=jnp.float32,
+        )
+        around = ((window.start, key_rows.shape[0] - window.stop), (0, 0), (0, 0))
+        key_grad = key_grad + jnp.pad(key_part, around)
+        value_grad = value_grad + jnp.pad(value_part, around)
+    return (key_grad, value_grad), jnp.stack(query_grads)
 
 
 def walk(place):
@@ -310,7 +272,6 @@
     heads_here = width_here // HEAD_DIM
     bounds = swap_places(clip_bounds) - (place - 1) * tokens
     bounds = bounds.reshape(2, -1, q_tile)
-    spans = jnp.stack([bounds[0, :, 0], bounds[1, :, -1]], axis=1)
 
     def head_blocks(value):
         return value.reshape(-1, q_tile, heads_here, HEAD_DIM)
@@ -332,7 +293,7 @@
         value_rows = kv[:, width_here:].reshape(-1, heads_here, HEAD_DIM)
         queries = contract(whole_one, w_qkv[:, :width_here], 0, 0) + own_bias[1]
         queries = head_blocks(queries.astype(jnp.bfloat16))
-        heads, logsum = attend_forward(queries, key_rows, value_rows, bounds, spans)
+        heads, logsum = attend_forward(queries, key_rows, value_rows, bounds)
         low_heads = heads.reshape(tokens, width_here).astype(jnp.bfloat16)
         w_other = other_weights[layer]
         w_up, w_down, w_out = (
@@ -419,7 +380,7 @@
         out_share = shared(contract(whole_grad, low_heads, 1, 0))
         inner_sums = jnp.sum(heads_grad.astype(jnp.float32) * heads, -1).transpose(0, 2, 1)
         (key_grad, value_grad), query_grad = attend_backward(
-            queries, heads_grad, inner_sums, logsum, key_rows, value_rows, bounds, spans
+            queries, heads_grad, inner_sums, logsum, key_rows, value_rows, bounds
         )
         kv_grad = jnp.concatenate(
             [

time: 1680 us -> 1310 us (0.78)
  loops' own time: 296 us -> 0 us
  local copies, waits for them, and re-layouts: 345 us -> 171 us
  matrix products: 256 us -> 421 us
  starting transfers between devices: 295 us -> 154 us
  other arithmetic: 148 us -> 203 us
  waiting for transfers between devices: 318 us -> 341 us
    another operation x16 -> x0, loops' own time: 296 us -> none  [the longest x12 171 us: by_window(): lax.switch(choice, [functools.partial(lambda size, *given: branch(size, j...]
    dot_general x30, matrix products: 131 us -> 305 us  [the longest x6 94.3 us: attend_backward(): jnp.einsum('qhd,khd->hqk', grads[i], values, preferred_element_type=jnp.f...]
    dynamic_update_slice x30 -> x0, local copies, waits for them, and re-layouts: 140 us -> none  [the longest x6 66 us: branch(): lax.dynamic_update_slice_in_dim(key_grad, key_part, first, 0)]
    ppermute x46, starting transfers between devices: 233 us -> 94.9 us  [swapped(): return lax.ppermute(value, axis, [(i, i ^ mask) for i in range(count)])]
    reduce_sum x6, other arithmetic: 13.3 us -> 51.9 us  [attend_forward(): total = jnp.sum(weights, -1, keepdims=True)]
    slice x22 -> x21, local copies, waits for them, and re-layouts: 27.3 us -> 56.9 us  [the longest x8 33.1 us: attend_forward(): key_rows[window]]
    squeeze x20 -> x0, local copies, waits for them, and re-layouts: 25.4 us -> none  [the longest x14 17.6 us: attend_forward(): return lax.map(one_block, (queries, bounds[0], bounds[1], spans))]
    dynamic_slice x30 -> x0, local copies, waits for them, and re-layouts: 22.3 us -> none  [the longest x24 17.8 us: attend_forward(): return lax.map(one_block, (queries, bounds[0], bounds[1], spans))]
  transfers between devices with their start and end apart: 103 -> 103, of which waited for: 55 -> 52; matrix products, arithmetic and copies ran while one was open for 21% -> 25% of each run, Pallas kernels for 0% -> 0%
where the time goes in v2:
time: 1310 us; the launch traced here: 1300 us
  matrix products  421 us (32%)
  waiting for transfers between devices  341 us (26%)
  other arithmetic  203 us (15%)
  local copies, waits for them, and re-layouts  171 us (13%)
  starting transfers between devices  154 us (12%)
    ppermute x46, waiting for transfers between devices, swapped(): return lax.ppermute(value, axis, [(i, i ^ mask) for i in range(count)])  142 us
    ppermute x32, waiting for transfers between devices, partner(): return lax.ppermute(value, 'narrow', [(i, i ^ mask) for i in range(4)])  134 us
    ppermute x46, starting transfers between devices, swapped(): return lax.ppermute(value, axis, [(i, i ^ mask) for i in range(count)])  94.9 us
    dot_general x6, matrix products, attend_backward(): jnp.einsum('qhd,khd->hqk', grads[i], values, preferred_element_type=jnp.f...  94.3 us
    dot_general x26, matrix products, contract(): lax.dot_general(left, right, (((left_dim,), (right_dim,)), ((), ())), pre...  79 us
    dot_general x6, matrix products, attend_forward(): jnp.einsum('hqk,khd->qhd', probabilities, value_rows[window], preferred_e...  72 us
    dot_general x6, matrix products, attend_backward(): jnp.einsum('hqk,qhd->khd', weights.astype(jnp.bfloat16), grads[i], prefer...  71.8 us
    ppermute x8, waiting for transfers between devices, along_path(): lax.ppermute(value, 'wide', [(walk(place), walk(place + step)) for place...  53.8 us
  transfers between devices with their start and end apart: 103, of which 52 were waited for; matrix products, arithmetic and copies ran while one was open for 25% of the time, Pallas kernels for 0%

profile of v2, /device:TPU:0, one launch (start us, length us, event | category | flops | bytes accessed | tf_op | source)
XLA Modules:
  0.0 1296.7 jit_solution(14684976604327003395)
XLA Ops:
  92.5 19.0 %collective-permute-done.6 = bf16[2,2,96,1728]{3,2,0,1:T(8,128)(2,1)S(1)} collective-permute-done((bf16[2,2,96,1728]{3,2,0,1:T(8,128)(2,1)S(1)}, bf16[2,2,96,1728]{3,2,0,1:T(8,128)(2,1)S(1)}, u32[]{:S(2)}, u32[]{:S(2)}) %collective-permute-start.6) | collective-permute-done | bytes 1327136 | tf_op jit(solution)/shard_map/ppermute | solution.py:137
  113.7 20.9 %collective-permute-done.18 = bf16[1536,384]{1,0:T(8,128)(2,1)S(1)} collective-permute-done((bf16[1536,384]{1,0:T(8,128)(2,1)S(1)}, bf16[1536,384]{1,0:T(8,128)(2,1)S(1)}, u32[]{:S(2)}, u32[]{:S(2)}) %collective-permute-start.18) | collective-permute-done | bytes 1179680 | tf_op jit(solution)/shard_map/ppermute | solution.py:92
  185.8 12.3 fusion.141
  213.0 12.0 fusion.140
  260.7 14.0 %collective-permute-done.21 = bf16[768,384]{1,0:T(8,128)(2,1)} collective-permute-done((bf16[768,384]{1,0:T(8,128)(2,1)S(1)}, bf16[768,384]{1,0:T(8,128)(2,1)}, u32[]{:S(2)}, u32[]{:S(2)}) %collective-permute-start.21) | collective-permute-done | bytes 589856 | tf_op jit(solution)/shard_map/ppermute | solution.py:103
  278.2 13.1 %collective-permute-done.22 = bf16[768,384]{1,0:T(8,128)(2,1)S(1)} collective-permute-done((bf16[768,384]{1,0:T(8,128)(2,1)S(1)}, bf16[768,384]{1,0:T(8,128)(2,1)S(1)}, u32[]{:S(2)}, u32[]{:S(2)}) %collective-permute-start.22) | collective-permute-done | bytes 589856 | tf_op jit(solution)/shard_map/ppermute | solution.py:103
  301.7 14.3 %fusion.65 = (bf16[768,1536]{1,0:T(8,128)(2,1)S(1)}, f32[768,1536]{1,0:T(8,128)}) fusion(f32[768]{0:T(1024)S(1)} %get-tuple-element.48, bf16[768,384]{1,0:T(8,128)(2,1)S(1)} %get-tuple-element.181, bf16[768,384]{1,0:T(8,128)(2,1)S(1)} %get-tuple-element.179, bf16[768,384]{1,0:T(8,128)(2,1)S(1)} %get-tuple-element.180, ...), kind=kOutput, calls=%fused_computation.97 | convolution fusion | flops 1899233280 | bytes 10620928 | tf_op jit(solution)/shard_map/dot_general | solution.py:14
  390.6 21.1 %collective-permute-done.28 = bf16[2,2,96,1728]{3,2,0,1:T(8,128)(2,1)S(1)} collective-permute-done((bf16[2,2,96,1728]{3,2,0,1:T(8,128)(2,1)S(1)}, bf16[2,2,96,1728]{3,2,0,1:T(8,128)(2,1)S(1)}, u32[]{:S(2)}, u32[]{:S(2)}) %collective-permute-start.28) | collective-permute-done | bytes 1327136 | tf_op jit(solution)/shard_map/ppermute | solution.py:137
  415.3 18.7 %collective-permute-done.35 = bf16[1536,384]{1,0:T(8,128)(2,1)S(1)} collective-permute-done((bf16[1536,384]{1,0:T(8,128)(2,1)S(1)}, bf16[1536,384]{1,0:T(8,128)(2,1)S(1)}, u32[]{:S(2)}, u32[]{:S(2)}) %collective-permute-start.35) | collective-permute-done | bytes 1179680 | tf_op jit(solution)/shard_map/ppermute | solution.py:92
  485.5 12.2 fusion.138
  512.6 12.1 fusion.137
  621.8 12.2 fusion.68
  694.1 18.3 %collective-permute-start.90 = (bf16[2,96,768]{2,1,0:T(8,128)(2,1)S(1)}, bf16[2,96,768]{2,1,0:T(8,128)(2,1)S(1)}, u32[]{:S(2)}, u32[]{:S(2)}) collective-permute-start(bf16[2,96,768]{2,1,0:T(8,128)(2,1)S(1)} %fusion.226), channel_id=1, source_target_pairs={{0,8},{4,12},{8,0},{12,4},{16,24},{20,28},{24,16},{28,20},{1,9},{5... | collective-permute-start | bytes 884744 | tf_op jit(solution)/shard_map/ppermute | solution.py:137
  753.2 12.0 fusion.51
  765.2 15.5 %multiply_convert_fusion.3 = bf16[3,512,3584]{2,1,0:T(8,128)(2,1)} fusion(f32[3,512,3584]{2,1,0:T(8,128)} %copy-done.23, bf16[512,3,64]{0,2,1:T(8,128)(2,1)S(1)} %bitcast.1169, bf16[3584,3,64]{0,2,1:T(8,128)(2,1)} %bitcast.1122, f32[3,512]{1,0:T(4,128)S(1)} %get-tuple-element.274, f32[3,512]{1,0:T(4,128)S(1)} %copy-done.232, pred[512,3584]{1,0:T(8,128)(4,1)S(1)} %copy-done.28), kind=kOutput, calls=%fused_computation.6 | convolution fusion | flops 737673216 | bytes 36450304 | tf_op jit(solution)/shard_map/qhd,khd->hqk/dot_general | solution.py:62
  791.3 12.0 fusion.45
  803.2 15.7 %multiply_convert_fusion.5 = bf16[3,512,3584]{2,1,0:T(8,128)(2,1)} fusion(f32[3,512,3584]{2,1,0:T(8,128)} %copy-done.22, bf16[512,3,64]{0,2,1:T(8,128)(2,1)S(1)} %bitcast.1165, bf16[3584,3,64]{0,2,1:T(8,128)(2,1)} %bitcast.1120, f32[3,512]{1,0:T(4,128)S(1)} %get-tuple-element.273, f32[3,512]{1,0:T(4,128)S(1)} %copy-done.231, pred[512,3584]{1,0:T(8,128)(4,1)} %fusion.42), kind=kOutput, calls=%fused_computation.10 | convolution fusion | flops 737673216 | bytes 36450304 | tf_op jit(solution)/shard_map/qhd,khd->hqk/dot_general | solution.py:62
  833.0 11.9 fusion.48
  845.0 16.0 %multiply_convert_fusion.4 = bf16[3,512,3584]{2,1,0:T(8,128)(2,1)} fusion(f32[3,512,3584]{2,1,0:T(8,128)} %copy-done.21, bf16[512,3,64]{0,2,1:T(8,128)(2,1)S(1)} %bitcast.1159, bf16[3584,3,64]{0,2,1:T(8,128)(2,1)} %bitcast.1118, f32[3,512]{1,0:T(4,128)S(1)} %get-tuple-element.275, f32[3,512]{1,0:T(4,128)S(1)} %copy-done.230, ...), kind=kOutput, calls=%fused_computation.8 | convolution fusion | flops 737673216 | bytes 36450304 | tf_op jit(solution)/shard_map/qhd,khd->hqk/dot_general | solution.py:62
  1058.8 12.0 fusion.60
  1070.7 15.4 %multiply_convert_fusion = bf16[3,512,3584]{2,1,0:T(8,128)(2,1)} fusion(f32[3,512,3584]{2,1,0:T(8,128)} %copy-done.20, bf16[512,3,64]{0,2,1:T(8,128)(2,1)S(1)} %bitcast.1167, bf16[3584,3,64]{0,2,1:T(8,128)(2,1)} %bitcast.1116, f32[3,512]{1,0:T(4,128)S(1)} %get-tuple-element.271, f32[3,512]{1,0:T(4,128)S(1)} %copy-done.229, pred[512,3584]{1,0:T(8,128)(4,1)S(1)} %copy-done.29), kind=kOutput, calls=%fused_computation | convolution fusion | flops 737673216 | bytes 36450304 | tf_op jit(solution)/shard_map/qhd,khd->hqk/dot_general | solution.py:62
  1108.6 16.0 %multiply_convert_fusion.2 = bf16[3,512,3584]{2,1,0:T(8,128)(2,1)} fusion(f32[3,512,3584]{2,1,0:T(8,128)} %copy-done.19, bf16[512,3,64]{0,2,1:T(8,128)(2,1)S(1)} %bitcast.1163, bf16[3584,3,64]{0,2,1:T(8,128)(2,1)} %bitcast.1114, f32[3,512]{1,0:T(4,128)S(1)} %get-tuple-element.270, f32[3,512]{1,0:T(4,128)S(1)} %copy-done.228, pred[512,3584]{1,0:T(8,128)(4,1)} %fusion.42), kind=kOutput, calls=%fused_computation.4 | convolution fusion | flops 737673216 | bytes 36450304 | tf_op jit(solution)/shard_map/qhd,khd->hqk/dot_general | solution.py:62
  1137.1 12.0 fusion.57
  1149.0 15.7 %multiply_convert_fusion.1 = bf16[3,512,3584]{2,1,0:T(8,128)(2,1)} fusion(f32[3,512,3584]{2,1,0:T(8,128)} %copy-done.18, bf16[512,3,64]{0,2,1:T(8,128)(2,1)S(1)} %bitcast.1161, bf16[3584,3,64]{0,2,1:T(8,128)(2,1)} %bitcast.1112, f32[3,512]{1,0:T(4,128)S(1)} %get-tuple-element.272, f32[3,512]{1,0:T(4,128)S(1)} %copy-done.227, ...), kind=kOutput, calls=%fused_computation.2 | convolution fusion | flops 737673216 | bytes 36450304 | tf_op jit(solution)/shard_map/qhd,khd->hqk/dot_general | solution.py:62
  (1162 shorter events, 936.8 us)
Async XLA Ops:
  10.3 32.6 %collective-permute-start.14 = (bf16[96,576]{0,1:T(8,128)(2,1)S(1)}, bf16[96,576]{0,1:T(8,128)(2,1)S(1)}, u32[]{:S(2)}, u32[]{:S(2)}) collective-permute-start(bf16[96,576]{0,1:T(8,128)(2,1)S(1)} %bitcast.1139), channel_id=1, source_target_pairs={{0,16},{4,20},{8,24},{12,28},{16,0},{20,4},{24,8},{28,12},{1,17},{... | collective-permute-start | bytes 331784 | tf_op jit(solution)/shard_map/ppermute | solution.py:137
  15.3 37.0 %collective-permute-start.4 = (bf16[96,1728]{1,0:T(8,128)(2,1)S(1)}, bf16[96,1728]{1,0:T(8,128)(2,1)S(1)}, u32[]{:S(2)}, u32[]{:S(2)}) collective-permute-start(bf16[96,1728]{1,0:T(8,128)(2,1)S(1)} %pad_maximum_fusion.66), channel_id=1, source_target_pairs={{0,16},{4,20},{8,24},{12,28},{16,0},{20,4},{24,8},{28,12},{1,17},{... | collective-permute-start | bytes 995336 | tf_op jit(solution)/shard_map/ppermute | solution.py:137
  18.4 25.6 %collective-permute-start.2 = (bf16[192,384]{1,0:T(8,128)(2,1)S(1)}, bf16[192,384]{1,0:T(8,128)(2,1)S(1)}, u32[]{:S(2)}, u32[]{:S(2)}) collective-permute-start(bf16[192,384]{1,0:T(8,128)(2,1)S(1)} %get-tuple-element.234), channel_id=1, source_target_pairs={{0,1},{1,0},{2,3},{3,2},{4,5},{5,4},{6,7},{7,6},{8,13},{9,12},{10,... | collective-permute-start | bytes 442376 | tf_op jit(solution)/shard_map/ppermute | solution.py:179
  25.2 24.7 %collective-permute-start.1 = (bf16[192,384]{1,0:T(8,128)(2,1)S(1)}, bf16[192,384]{1,0:T(8,128)(2,1)S(1)}, u32[]{:S(2)}, u32[]{:S(2)}) collective-permute-start(bf16[192,384]{1,0:T(8,128)(2,1)S(1)} %get-tuple-element.235), channel_id=1, source_target_pairs={{0,2},{1,3},{2,0},{3,1},{4,6},{5,7},{6,4},{7,5},{8,14},{9,15},{10,... | collective-permute-start | bytes 442376 | tf_op jit(solution)/shard_map/ppermute | solution.py:179
  78.4 33.2 %collective-permute-start.6 = (bf16[2,2,96,1728]{3,2,0,1:T(8,128)(2,1)S(1)}, bf16[2,2,96,1728]{3,2,0,1:T(8,128)(2,1)S(1)}, u32[]{:S(2)}, u32[]{:S(2)}) collective-permute-start(bf16[2,2,96,1728]{3,2,0,1:T(8,128)(2,1)S(1)} %pad_maximum_fusion.31), channel_id=1, source_target_pairs={{0,4},{4,0},{8,12},{12,8},{16,20},{20,16},{24,28},{28,24},{1,5},{5... | collective-permute-start | bytes 3981320 | tf_op jit(solution)/shard_map/ppermute | solution.py:137
  84.7 49.9 %collective-permute-start.18 = (bf16[1536,384]{1,0:T(8,128)(2,1)S(1)}, bf16[1536,384]{1,0:T(8,128)(2,1)S(1)}, u32[]{:S(2)}, u32[]{:S(2)}) collective-permute-start(bf16[1536,384]{1,0:T(8,128)(2,1)S(1)} %fusion.95), channel_id=1, source_target_pairs={{4,0},{12,4},{8,12},{16,8},{20,16},{28,20},{24,28},{5,1},{13,5},{9... | collective-permute-start | bytes 3538952 | tf_op jit(solution)/shard_map/ppermute | solution.py:92
  86.0 48.6 %collective-permute-start.17 = (bf16[1536,384]{1,0:T(8,128)(2,1)S(1)}, bf16[1536,384]{1,0:T(8,128)(2,1)S(1)}, u32[]{:S(2)}, u32[]{:S(2)}) collective-permute-start(bf16[1536,384]{1,0:T(8,128)(2,1)S(1)} %fusion.95), channel_id=1, source_target_pairs={{0,4},{4,12},{12,8},{8,16},{16,20},{20,28},{28,24},{1,5},{5,13},{1... | collective-permute-start | bytes 3538952 | tf_op jit(solution)/shard_map/ppermute | solution.py:92
  378.5 33.2 %collective-permute-start.28 = (bf16[2,2,96,1728]{3,2,0,1:T(8,128)(2,1)S(1)}, bf16[2,2,96,1728]{3,2,0,1:T(8,128)(2,1)S(1)}, u32[]{:S(2)}, u32[]{:S(2)}) collective-permute-start(bf16[2,2,96,1728]{3,2,0,1:T(8,128)(2,1)S(1)} %pad_maximum_fusion.32), channel_id=1, source_target_pairs={{0,4},{4,0},{8,12},{12,8},{16,20},{20,16},{24,28},{28,24},{1,5},{5... | collective-permute-start | bytes 3981320 | tf_op jit(solution)/shard_map/ppermute | solution.py:137
  384.7 49.4 %collective-permute-start.35 = (bf16[1536,384]{1,0:T(8,128)(2,1)S(1)}, bf16[1536,384]{1,0:T(8,128)(2,1)S(1)}, u32[]{:S(2)}, u32[]{:S(2)}) collective-permute-start(bf16[1536,384]{1,0:T(8,128)(2,1)S(1)} %fusion.96), channel_id=1, source_target_pairs={{4,0},{12,4},{8,12},{16,8},{20,16},{28,20},{24,28},{5,1},{13,5},{9... | collective-permute-start | bytes 3538952 | tf_op jit(solution)/shard_map/ppermute | solution.py:92
  386.0 48.1 %collective-permute-start.34 = (bf16[1536,384]{1,0:T(8,128)(2,1)S(1)}, bf16[1536,384]{1,0:T(8,128)(2,1)S(1)}, u32[]{:S(2)}, u32[]{:S(2)}) collective-permute-start(bf16[1536,384]{1,0:T(8,128)(2,1)S(1)} %fusion.96), channel_id=1, source_target_pairs={{0,4},{4,12},{12,8},{8,16},{16,20},{20,28},{28,24},{1,5},{5,13},{1... | collective-permute-start | bytes 3538952 | tf_op jit(solution)/shard_map/ppermute | solution.py:92
  569.2 23.5 %collective-permute-start.37 = (bf16[768,384]{1,0:T(8,128)(2,1)}, bf16[768,384]{1,0:T(8,128)(2,1)}, u32[]{:S(2)}, u32[]{:S(2)}) collective-permute-start(bf16[768,384]{1,0:T(8,128)(2,1)} %fusion.184), channel_id=1, source_target_pairs={{0,2},{1,3},{2,0},{3,1},{4,6},{5,7},{6,4},{7,5},{8,10},{9,11},{10,... | collective-permute-start | bytes 1769480 | tf_op jit(solution)/shard_map/ppermute | solution.py:103
  649.1 21.0 %collective-permute-start.40 = (bf16[2,768,384]{2,1,0:T(8,128)(2,1)}, bf16[2,768,384]{2,1,0:T(8,128)(2,1)}, u32[]{:S(2)}, u32[]{:S(2)}) collective-permute-start(bf16[2,768,384]{2,1,0:T(8,128)(2,1)} %select_convert_fusion.4), channel_id=1, source_target_pairs={{0,1},{1,0},{2,3},{3,2},{4,5},{5,4},{6,7},{7,6},{8,9},{9,8},{10,11... | collective-permute-start | bytes 3538952 | tf_op jit(solution)/shard_map/ppermute | solution.py:103
  658.6 56.2 %collective-permute-start.95 = (bf16[4,96,768]{2,1,0:T(8,128)(2,1)}, bf16[4,96,768]{2,1,0:T(8,128)(2,1)S(1)}, u32[]{:S(2)}, u32[]{:S(2)}) collective-permute-start(bf16[4,96,768]{2,1,0:T(8,128)(2,1)} %fusion.193), channel_id=1, source_target_pairs={{0,4},{4,0},{8,12},{12,8},{16,20},{20,16},{24,28},{28,24},{1,5},{5... | collective-permute-start | bytes 1769480 | tf_op jit(solution)/shard_map/ppermute | solution.py:137
  691.2 21.2 %collective-permute-start.42 = (bf16[192,384]{1,0:T(8,128)(2,1)S(1)}, bf16[192,384]{1,0:T(8,128)(2,1)S(1)}, u32[]{:S(2)}, u32[]{:S(2)}) collective-permute-start(bf16[192,384]{1,0:T(8,128)(2,1)S(1)} %get-tuple-element.219), channel_id=1, source_target_pairs={{0,3},{1,2},{2,1},{3,0},{4,7},{5,6},{6,5},{7,4},{8,15},{9,14},{10,... | collective-permute-start | bytes 442376 | tf_op jit(solution)/shard_map/ppermute | solution.py:179
  694.1 34.2 %collective-permute-start.90 = (bf16[2,96,768]{2,1,0:T(8,128)(2,1)S(1)}, bf16[2,96,768]{2,1,0:T(8,128)(2,1)S(1)}, u32[]{:S(2)}, u32[]{:S(2)}) collective-permute-start(bf16[2,96,768]{2,1,0:T(8,128)(2,1)S(1)} %fusion.226), channel_id=1, source_target_pairs={{0,8},{4,12},{8,0},{12,4},{16,24},{20,28},{24,16},{28,20},{1,9},{5... | collective-permute-start | bytes 884744 | tf_op jit(solution)/shard_map/ppermute | solution.py:137
  731.6 186.7 %collective-permute-start.97 = (bf16[1,96,768]{2,1,0:T(8,128)(2,1)}, bf16[1,96,768]{2,1,0:T(8,128)(2,1)}, u32[]{:S(2)}, u32[]{:S(2)}) collective-permute-start(bf16[1,96,768]{2,1,0:T(8,128)(2,1)} %fusion.238), channel_id=1, source_target_pairs={{0,16},{4,20},{8,24},{12,28},{16,0},{20,4},{24,8},{28,12},{1,17},{... | collective-permute-start | bytes 442376 | tf_op jit(solution)/shard_map/ppermute | solution.py:137
  832.4 57.0 %collective-permute-start.83 = (bf16[4,96,192]{2,1,0:T(8,128)(2,1)S(1)}, bf16[4,96,192]{2,1,0:T(8,128)(2,1)S(1)}, u32[]{:S(2)}, u32[]{:S(2)}) collective-permute-start(bf16[4,96,192]{2,1,0:T(8,128)(2,1)S(1)} %fusion.232), channel_id=1, source_target_pairs={{0,4},{4,0},{8,12},{12,8},{16,20},{20,16},{24,28},{28,24},{1,5},{5... | collective-permute-start | bytes 442376 | tf_op jit(solution)/shard_map/ppermute | solution.py:137
  878.2 23.3 %collective-permute-start.56 = (bf16[1536,384]{0,1:T(8,128)(2,1)}, bf16[1536,384]{0,1:T(8,128)(2,1)}, u32[]{:S(2)}, u32[]{:S(2)}) collective-permute-start(bf16[1536,384]{0,1:T(8,128)(2,1)} %get-tuple-element.103), channel_id=1, source_target_pairs={{4,0},{12,4},{8,12},{16,8},{20,16},{28,20},{24,28},{5,1},{13,5},{9... | collective-permute-start | bytes 3538952 | tf_op jit(solution)/shard_map/ppermute | solution.py:92
  879.5 23.3 %collective-permute-start.57 = (bf16[1536,384]{0,1:T(8,128)(2,1)}, bf16[1536,384]{0,1:T(8,128)(2,1)}, u32[]{:S(2)}, u32[]{:S(2)}) collective-permute-start(bf16[1536,384]{0,1:T(8,128)(2,1)} %get-tuple-element.104), channel_id=1, source_target_pairs={{0,4},{4,12},{12,8},{8,16},{16,20},{20,28},{28,24},{1,5},{5,13},{1... | collective-permute-start | bytes 3538952 | tf_op jit(solution)/shard_map/ppermute | solution.py:92
  908.7 22.9 %collective-permute-start.58 = (bf16[2,768,384]{2,1,0:T(8,128)(2,1)}, bf16[2,768,384]{2,1,0:T(8,128)(2,1)}, u32[]{:S(2)}, u32[]{:S(2)}) collective-permute-start(bf16[2,768,384]{2,1,0:T(8,128)(2,1)} %select_convert_fusion.2), channel_id=1, source_target_pairs={{0,1},{1,0},{2,3},{3,2},{4,5},{5,4},{6,7},{7,6},{8,9},{9,8},{10,11... | collective-permute-start | bytes 3538952 | tf_op jit(solution)/shard_map/ppermute | solution.py:103
  994.2 22.7 %collective-permute-start.86 = (bf16[4,96,768]{2,1,0:T(8,128)(2,1)S(1)}, bf16[4,96,768]{2,1,0:T(8,128)(2,1)S(1)}, u32[]{:S(2)}, u32[]{:S(2)}) collective-permute-start(bf16[4,96,768]{2,1,0:T(8,128)(2,1)S(1)} %fusion.190), channel_id=1, source_target_pairs={{0,4},{4,0},{8,12},{12,8},{16,20},{20,16},{24,28},{28,24},{1,5},{5... | collective-permute-start | bytes 1769480 | tf_op jit(solution)/shard_map/ppermute | solution.py:137
  1184.6 29.8 %collective-permute-start.66 = (bf16[1536,384]{0,1:T(8,128)(2,1)}, bf16[1536,384]{0,1:T(8,128)(2,1)}, u32[]{:S(2)}, u32[]{:S(2)}) collective-permute-start(bf16[1536,384]{0,1:T(8,128)(2,1)} %get-tuple-element.101), channel_id=1, source_target_pairs={{4,0},{12,4},{8,12},{16,8},{20,16},{28,20},{24,28},{5,1},{13,5},{9... | collective-permute-start | bytes 3538952 | tf_op jit(solution)/shard_map/ppermute | solution.py:92
  1185.9 29.7 %collective-permute-start.67 = (bf16[1536,384]{0,1:T(8,128)(2,1)}, bf16[1536,384]{0,1:T(8,128)(2,1)}, u32[]{:S(2)}, u32[]{:S(2)}) collective-permute-start(bf16[1536,384]{0,1:T(8,128)(2,1)} %get-tuple-element.102), channel_id=1, source_target_pairs={{0,4},{4,12},{12,8},{8,16},{16,20},{20,28},{28,24},{1,5},{5,13},{1... | collective-permute-start | bytes 3538952 | tf_op jit(solution)/shard_map/ppermute | solution.py:92
  1203.0 37.6 %collective-permute-start.82 = (bf16[1,96,192]{1,2,0:T(8,128)(2,1)S(1)}, bf16[1,96,192]{1,2,0:T(8,128)(2,1)S(1)}, u32[]{:S(2)}, u32[]{:S(2)}) collective-permute-start(bf16[1,96,192]{1,2,0:T(8,128)(2,1)S(1)} %fusion.243), channel_id=1, source_target_pairs={{0,16},{4,20},{8,24},{12,28},{16,0},{20,4},{24,8},{28,12},{1,17},{... | collective-permute-start | bytes 110600 | tf_op jit(solution)/shard_map/ppermute | solution.py:137
  (323 other events, 3417.6 us)
